TPU v7x, 768 devices: a whole 4x8x12 slice. The times are simulated.
768 devices in a mesh: dp: 64 (over x, y, core), mp: 12 (over z).
Axes of the slice: x: 4, y: 8, z: 12, core: 2. Of those that a mesh axis runs over, the one named last changes fastest.
Arguments:
- inputs: bfloat16 [128, 48, 4096], P('dp')
- denoiser: int32 [128], P('dp'), may hold values from 0 to 2
- span_mask: int32 [128, 48], P('dp'), may hold values 0 or 1
- lengths: int32 [128], P('dp'), may hold values from 12 to 48
- move_plan: int32 [128], P('dp'), may hold values from -1 to 1, as said below
- mode_table: bfloat16 [3, 4096], replicated, may hold values from -3 to 3
- sentinel: bfloat16 [4096], replicated, may hold values from -6 to 6
- w_query: bfloat16 [4096, 3072], P(None, 'mp')
- w_key: bfloat16 [4096, 3072], P(None, 'mp')
- w_value: bfloat16 [4096, 3072], P(None, 'mp'), may hold values from -0.09375 to 0.09375
- cotangent: bfloat16 [256, 48, 3072], P('dp', None, 'mp'), may hold values from -6 to 6
Outputs:
- context: bfloat16 [256, 48, 3072], P('dp', None, 'mp')
- input_grad: bfloat16 [128, 48, 4096], P('dp', 'mp')
Inputs may be any that keep to these rules, and one draw needn't show every extreme that they name: `move_plan`: every row stays (0) or moves to the next (1) or previous (-1) data group along dp, cyclically. A data group sends at most one row to each of its two neighbours, and in every draw some data group receives a row from both neighbours.
All inputs are finite; a program needn't handle non-finite values. No bound on the sum of `span_mask` on one device may be relied on, other than what follows from the above.
Results may differ from a plain program's by a relative error of at most 0.02.
The roundings to bfloat16 on the way count: a program that leaves them out, or rounds other values in their place, can miss the bound.
Values may be sent and summed in bfloat16 or wider, within the bound.
No kernel may reach another device: no remote copies, remote signals or barrier semaphores. Data moves between devices by JAX's collectives and lax.ppermute only.
A program may use at most 64 MiB of HBM per device.

v0:
```python
import math

import jax
import jax.numpy as jnp
from jax import lax
from jax.sharding import PartitionSpec as P


def shifted(array, axis, by):
    devices = lax.axis_size(axis)
    return lax.ppermute(array, axis, [(i, (i + by) % devices) for i in range(devices)])


def attend(slot_rows, slot_len, cotangent, w_query, w_key, w_value):
    slot_count, length, model_width = slot_rows.shape
    head_size = w_query.shape[1]
    flat_rows = slot_rows.astype(jnp.float32).reshape(slot_count * length, model_width)
    inv_rms = lax.rsqrt(jnp.mean(flat_rows * flat_rows, axis=1, keepdims=True) + 1e-06)
    normed = flat_rows * inv_rms
    normed_b = normed.astype(jnp.bfloat16)

    def project(weight):
        result = jnp.dot(normed_b, weight, preferred_element_type=jnp.float32)
        return result.astype(jnp.bfloat16).reshape(slot_count, length, head_size)

    query_rows = project(w_query)
    key_rows = project(w_key)
    value_rows = project(w_value)
    positions = jnp.arange(length, dtype=jnp.int32)
    key_ok = positions[None, None, :] < jnp.maximum(slot_len, 1)[:, None, None]
    query_ok = positions[None, :, None] < slot_len[:, None, None]
    factor = 1.0 / math.sqrt(head_size)
    scores = (
        jnp.einsum("sqd,skd->sqk", query_rows, key_rows, preferred_element_type=jnp.float32)
        * factor
    )
    scores = jnp.where(key_ok, scores, -jnp.inf)
    row_max = jnp.max(scores, axis=2, keepdims=True)
    exp_scores = jnp.exp(scores - row_max)
    soft = exp_scores / jnp.sum(exp_scores, axis=2, keepdims=True)
    soft_b = soft.astype(jnp.bfloat16)
    context = jnp.einsum("sqk,skd->sqd", soft_b, value_rows, preferred_element_type=jnp.float32)
    context = (context * query_ok.astype(jnp.float32)).astype(jnp.bfloat16)
    grad_out = jnp.where(query_ok, cotangent, jnp.zeros_like(cotangent))
    grad_value = jnp.einsum(
        "sqk,sqd->skd", soft_b, grad_out, preferred_element_type=jnp.float32
    ).astype(jnp.bfloat16)
    grad_soft = jnp.einsum("sqd,skd->sqk", grad_out, value_rows, preferred_element_type=jnp.float32)
    row_inner = jnp.sum(soft * grad_soft, axis=2, keepdims=True)
    grad_scores = (soft * (grad_soft - row_inner) * factor).astype(jnp.bfloat16)
    grad_query = jnp.einsum(
        "sqk,skd->sqd", grad_scores, key_rows, preferred_element_type=jnp.float32
    ).astype(jnp.bfloat16)
    grad_key = jnp.einsum(
        "sqk,sqd->skd", grad_scores, query_rows, preferred_element_type=jnp.float32
    ).astype(jnp.bfloat16)

    def project_back(gradient, weight):
        flat_grad = gradient.reshape(slot_count * length, head_size)
        return lax.dot_general(
            flat_grad, weight, (((1,), (1,)), ((), ())), preferred_element_type=jnp.float32
        )

    head_grad = (
        project_back(grad_query, w_query)
        + project_back(grad_key, w_key)
        + project_back(grad_value, w_value)
    )
    inner_norm = jnp.mean(head_grad * normed, axis=1, keepdims=True)
    head_part = ((head_grad - normed * inner_norm) * inv_rms).astype(jnp.bfloat16)
    return (context, head_part.reshape(slot_count, length, model_width))


def shards(
    inputs,
    denoiser,
    span_mask,
    lengths,
    move_plan,
    mode_table,
    sentinel,
    w_query,
    w_key,
    w_value,
    cotangent,
):
    rows_dev, length, model_width = inputs.shape
    seg_rows = length // lax.axis_size("mp")
    offset_start = lax.axis_index("mp") * seg_rows
    mode_count = mode_table.shape[0]
    picked = (denoiser[:, None] == jnp.arange(mode_count, dtype=jnp.int32)[None, :]).astype(
        jnp.float32
    )
    mode_rows = jnp.sum(picked[:, :, None] * mode_table.astype(jnp.float32)[None, :, :], axis=1)
    span_flag = (span_mask == 1)[:, :, None]
    shaped = jnp.where(
        span_flag,
        sentinel.astype(jnp.float32)[None, None, :],
        inputs.astype(jnp.float32) + mode_rows[:, None, :],
    ).astype(jnp.bfloat16)
    goes_right = move_plan == 1
    goes_left = move_plan == -1
    stays = move_plan == 0

    def outgoing(flags):
        chosen = jnp.argmax(flags.astype(jnp.int32))
        picked_row = jnp.where(jnp.any(flags), shaped[chosen], jnp.zeros_like(shaped[0]))
        picked_len = jnp.sum(jnp.where(flags, lengths, 0)).reshape(1)
        return (picked_row, picked_len)

    right_rows, right_len = outgoing(goes_right)
    left_rows, left_len = outgoing(goes_left)

    def carry_whole(payload, offset):
        return shifted((payload[0], payload[1]), "dp", offset)

    from_left_rows, from_left_len = carry_whole((right_rows, right_len), 1)
    from_right_rows, from_right_len = carry_whole((left_rows, left_len), -1)
    arrived = jnp.stack([from_left_rows, from_right_rows])
    slot_rows = jnp.concatenate([shaped, arrived], axis=0)
    slot_len = jnp.concatenate(
        [jnp.where(stays, lengths, 0), from_left_len, from_right_len]
    ).astype(jnp.int32)
    context, head_part = attend(slot_rows, slot_len, cotangent, w_query, w_key, w_value)
    span_piece = lax.dynamic_slice_in_dim(span_mask, offset_start, seg_rows, 1)

    def carry_part(payload, offset):
        return shifted(payload, "dp", offset)

    back_right = carry_part(head_part[rows_dev], -1)
    back_left = carry_part(head_part[rows_dev + 1], 1)
    own_rows = head_part[:rows_dev]
    merged = jnp.where(
        stays[:, None, None],
        own_rows,
        jnp.where(
            goes_right[:, None, None],
            back_right[None, :, :],
            jnp.where(goes_left[:, None, None], back_left[None, :, :], jnp.zeros_like(own_rows)),
        ),
    )
    summed = lax.psum_scatter(
        merged.astype(jnp.float32).astype(jnp.bfloat16), "mp", scatter_dimension=1, tiled=True
    )
    input_grad = jnp.where((span_piece == 1)[:, :, None], jnp.zeros_like(summed), summed)
    return (context, input_grad)


def solution(mesh):
    return jax.shard_map(
        shards,
        mesh=mesh,
        in_specs=(
            P("dp", None, None),
            P("dp"),
            P("dp", None),
            P("dp"),
            P("dp"),
            P(),
            P(),
            P(None, "mp"),
            P(None, "mp"),
            P(None, "mp"),
            P("dp", None, "mp"),
        ),
        out_specs=(P("dp", None, "mp"), P("dp", "mp", None)),
        check_vma=False,
    )
```

profile of v0, /device:TPU:56, one launch (start us, length us, event | category | flops | bytes accessed | tf_op | source)
XLA Modules:
  0.0 201.3 jit_solution(4572477801767732647)
XLA Ops:
  7.2 1.4 iota_reduce_fusion
  8.7 1.3 iota_reduce_fusion.1
  12.4 1.4 fusion.32
  13.8 0.7 broadcast_compare_fusion
  14.5 0.7 fusion.21
  15.1 0.8 convert_element_type.81
  17.2 1.4 select_convert_fusion
  18.6 1.4 select_bitcast_fusion.1
  20.0 1.9 collective-permute-start.2
  21.9 3.6 %collective-permute-start.3 = (bf16[48,4096]{1,0:T(8,128)(2,1)S(1)}, bf16[48,4096]{1,0:T(8,128)(2,1)S(1)}, u32[]{:S(2)}, u32[]{:S(2)}) collective-permute-start(bf16[48,4096]{1,0:T(8,128)(2,1)S(1)} %get-tuple-element.15), channel_id=1, source_target_pairs={{0,756},{12,0},{24,12},{36,24},{48,36},{60,48},{72,60},{84,72},{96... | collective-permute-start | bytes 1179656 | tf_op jit(solution)/shard_map/ppermute | solution.py:11
  26.2 1.9 collective-permute-start
  28.1 3.6 %collective-permute-start.1 = (s32[1]{0:T(128)}, s32[1]{0:T(128)}, u32[]{:S(2)}, u32[]{:S(2)}) collective-permute-start(s32[1]{0:T(128)} %bitcast.1), channel_id=1, source_target_pairs={{0,756},{12,0},{24,12},{36,24},{48,36},{60,48},{72,60},{84,72},{96... | collective-permute-start | bytes 20 | tf_op jit(solution)/shard_map/ppermute | solution.py:11
  31.8 1.9 collective-permute-done.1
  33.7 1.3 broadcast_maximum_fusion
  35.5 1.9 maximum_convert_fusion
  37.5 2.4 %bitcast_multiply_fusion = f32[192,4096]{1,0:T(8,128)S(1)} fusion(f32[4,48,4096]{2,1,0:T(8,128)} %maximum_convert_fusion, f32[192]{0:T(256)S(1)} %rsqrt.12), kind=kLoop, calls=%fused_computation.4 | loop fusion | flops 786432 | bytes 6292224 | tf_op jit(solution)/shard_map/mul | solution.py:19
  40.6 2.1 %copy-done.5 = bf16[4096,256]{1,0:T(8,128)(2,1)S(1)} copy-done((bf16[4096,256]{1,0:T(8,128)(2,1)S(1)}, bf16[4096,256]{1,0:T(8,128)(2,1)}, u32[]{:S(2)}) %copy-start.5) | copy-done | bytes 2097176
  43.3 0.9 copy-done.4
  46.1 2.6 %fusion.36 = f32[192,4096]{1,0:T(8,128)S(1)} fusion(bf16[192,256]{1,0:T(8,128)(2,1)S(1)} %bitcast.53, bf16[4096,256]{1,0:T(8,128)(2,1)} %param.18), kind=kOutput, calls=%fused_computation.75 | convolution fusion | flops 402653184 | bytes 5341184 | tf_op jit(solution)/shard_map/dot_general | solution.py:60
  48.7 0.9 convolution_add_fusion.1
  49.6 1.0 copy-done.2
  50.6 1.1 multiply_reduce_fusion
  51.7 0.8 copy-done.3
  52.5 0.9 multiply_convert_fusion
  53.5 3.2 %collective-permute-start.4 = (bf16[48,4096]{1,0:T(8,128)(2,1)S(1)}, bf16[48,4096]{1,0:T(8,128)(2,1)S(1)}, u32[]{:S(2)}, u32[]{:S(2)}) collective-permute-start(bf16[48,4096]{1,0:T(8,128)(2,1)S(1)} %get-tuple-element.12), channel_id=1, source_target_pairs={{0,756},{12,0},{24,12},{36,24},{48,36},{60,48},{72,60},{84,72},{96... | collective-permute-start | bytes 1179656 | tf_op jit(solution)/shard_map/ppermute | solution.py:11
  56.7 5.2 %collective-permute-start.5 = (bf16[48,4096]{1,0:T(8,128)(2,1)S(1)}, bf16[48,4096]{1,0:T(8,128)(2,1)S(1)}, u32[]{:S(2)}, u32[]{:S(2)}) collective-permute-start(bf16[48,4096]{1,0:T(8,128)(2,1)S(1)} %get-tuple-element.13), channel_id=1, source_target_pairs={{0,12},{12,24},{24,36},{36,48},{48,60},{60,72},{72,84},{84,96},{96... | collective-permute-start | bytes 1179656 | tf_op jit(solution)/shard_map/ppermute | solution.py:11
  62.0 3.8 %collective-permute-done.5 = bf16[48,4096]{1,0:T(8,128)(2,1)S(1)} collective-permute-done((bf16[48,4096]{1,0:T(8,128)(2,1)S(1)}, bf16[48,4096]{1,0:T(8,128)(2,1)S(1)}, u32[]{:S(2)}, u32[]{:S(2)}) %collective-permute-start.5) | collective-permute-done | bytes 393248 | tf_op jit(solution)/shard_map/ppermute | solution.py:11
  65.8 1.1 select_select_fusion
  66.9 1.3 dynamic-slice
  68.9 0.9 fusion.3
  69.8 123.0 %all-reduce.3.cloned.1.call-done = bf16[2,48,4096]{2,1,0:T(8,128)(2,1)} async-done(((bf16[2,48,4096]{2,1,0:T(8,128)(2,1)}), bf16[2,48,4096]{2,1,0:T(8,128)(2,1)}) %all-reduce.3.cloned.1.call-update) | async-done | bytes 786448
  192.8 1.6 dynamic-slice_select_fusion
  (43 shorter events, 4.8 us)
Async XLA Ops:
  7.2 32.7 %copy-start = (bf16[4096,256]{1,0:T(8,128)(2,1)S(1)}, bf16[4096,256]{1,0:T(8,128)(2,1)}, u32[]{:S(2)}) copy-start(bf16[4096,256]{1,0:T(8,128)(2,1)} %param.20) | copy-start | bytes 6291460
  7.2 18.4 %copy-start.8 = (s32[2]{0:T(128)S(1)}, s32[2]{0:T(128)}, u32[]{:S(2)}) copy-start(s32[2]{0:T(128)} %param.15) | copy-start | bytes 28
  7.2 18.4 %copy-start.10 = (s32[2]{0:T(128)S(1)}, s32[2]{0:T(128)}, u32[]{:S(2)}) copy-start(s32[2]{0:T(128)} %param.14) | copy-start | bytes 28
  7.2 185.6 %all-reduce.3.cloned.1.call-start = ((), (), s32[]{:S(2)}) async-start(), calls=%async_computation | async-start | bytes 1572864
  20.0 15.1 %collective-permute-start.2 = (bf16[48,4096]{1,0:T(8,128)(2,1)S(1)}, bf16[48,4096]{1,0:T(8,128)(2,1)S(1)}, u32[]{:S(2)}, u32[]{:S(2)}) collective-permute-start(bf16[48,4096]{1,0:T(8,128)(2,1)S(1)} %get-tuple-element.14), channel_id=1, source_target_pairs={{0,12},{12,24},{24,36},{36,48},{48,60},{60,72},{72,84},{84,96},{96... | collective-permute-start | bytes 1179656 | tf_op jit(solution)/shard_map/ppermute | solution.py:11
  21.9 13.2 %collective-permute-start.3 = (bf16[48,4096]{1,0:T(8,128)(2,1)S(1)}, bf16[48,4096]{1,0:T(8,128)(2,1)S(1)}, u32[]{:S(2)}, u32[]{:S(2)}) collective-permute-start(bf16[48,4096]{1,0:T(8,128)(2,1)S(1)} %get-tuple-element.15), channel_id=1, source_target_pairs={{0,756},{12,0},{24,12},{36,24},{48,36},{60,48},{72,60},{84,72},{96... | collective-permute-start | bytes 1179656 | tf_op jit(solution)/shard_map/ppermute | solution.py:11
  26.2 5.6 %collective-permute-start = (s32[1]{0:T(128)}, s32[1]{0:T(128)}, u32[]{:S(2)}, u32[]{:S(2)}) collective-permute-start(s32[1]{0:T(128)} %bitcast), channel_id=1, source_target_pairs={{0,12},{12,24},{24,36},{36,48},{48,60},{60,72},{72,84},{84,96},{96... | collective-permute-start | bytes 20 | tf_op jit(solution)/shard_map/ppermute | solution.py:11
  28.1 5.5 %collective-permute-start.1 = (s32[1]{0:T(128)}, s32[1]{0:T(128)}, u32[]{:S(2)}, u32[]{:S(2)}) collective-permute-start(s32[1]{0:T(128)} %bitcast.1), channel_id=1, source_target_pairs={{0,756},{12,0},{24,12},{36,24},{48,36},{60,48},{72,60},{84,72},{96... | collective-permute-start | bytes 20 | tf_op jit(solution)/shard_map/ppermute | solution.py:11
  39.9 3.4 %copy-start.1 = (f32[192,4096]{1,0:T(8,128)}, f32[192,4096]{1,0:T(8,128)S(1)}, u32[]{:S(2)}) copy-start(f32[192,4096]{1,0:T(8,128)S(1)} %bitcast_multiply_fusion) | copy-start | bytes 9437188
  39.9 2.7 %copy-start.5 = (bf16[4096,256]{1,0:T(8,128)(2,1)S(1)}, bf16[4096,256]{1,0:T(8,128)(2,1)}, u32[]{:S(2)}) copy-start(bf16[4096,256]{1,0:T(8,128)(2,1)} %param.19) | copy-start | bytes 6291460
  42.6 1.6 copy-start.4
  44.2 1.0 copy-start.7
  46.1 2.6 %copy-start.6 = (bf16[4096,256]{1,0:T(8,128)(2,1)S(1)}, bf16[4096,256]{1,0:T(8,128)(2,1)}, u32[]{:S(2)}) copy-start(bf16[4096,256]{1,0:T(8,128)(2,1)} %param.19) | copy-start | bytes 6291460
  48.7 1.9 copy-start.2
  50.6 1.9 copy-start.3
  53.5 8.5 %collective-permute-start.4 = (bf16[48,4096]{1,0:T(8,128)(2,1)S(1)}, bf16[48,4096]{1,0:T(8,128)(2,1)S(1)}, u32[]{:S(2)}, u32[]{:S(2)}) collective-permute-start(bf16[48,4096]{1,0:T(8,128)(2,1)S(1)} %get-tuple-element.12), channel_id=1, source_target_pairs={{0,756},{12,0},{24,12},{36,24},{48,36},{60,48},{72,60},{84,72},{96... | collective-permute-start | bytes 1179656 | tf_op jit(solution)/shard_map/ppermute | solution.py:11
  56.7 12.2 %copy-start.9 = (s32[2,48]{1,0:T(2,128)S(1)}, s32[2,48]{1,0:T(2,128)}, u32[]{:S(2)}) copy-start(s32[2,48]{1,0:T(2,128)} %param.13) | copy-start | bytes 1156
  56.7 9.1 %collective-permute-start.5 = (bf16[48,4096]{1,0:T(8,128)(2,1)S(1)}, bf16[48,4096]{1,0:T(8,128)(2,1)S(1)}, u32[]{:S(2)}, u32[]{:S(2)}) collective-permute-start(bf16[48,4096]{1,0:T(8,128)(2,1)S(1)} %get-tuple-element.13), channel_id=1, source_target_pairs={{0,12},{12,24},{24,36},{36,48},{48,60},{60,72},{72,84},{84,96},{96... | collective-permute-start | bytes 1179656 | tf_op jit(solution)/shard_map/ppermute | solution.py:11
Sparse Core Ops, SparseCore 0:
  67.0 125.7 all-reduce.2
where the time goes:
time: 203 us; the launch traced here: 201 us
  waiting for transfers between devices  129 us (64%)
  other arithmetic  19.7 us (10%)
  starting transfers between devices  19.6 us (10%)
  between operations  18.6 us (9%)
  matrix products  8.37 us (4%)
  local copies, waits for them, and re-layouts  6.32 us (3%)
    unnamed x2, waiting for transfers between devices  123 us
    ppermute x6, starting transfers between devices, shifted(): lax.ppermute(array, axis, [(i, (i + by) % devices) for i in range(devices)])  19.5 us
    unnamed x23, local copies, waits for them, and re-layouts  6.13 us
    ppermute x6, waiting for transfers between devices, shifted(): lax.ppermute(array, axis, [(i, (i + by) % devices) for i in range(devices)])  5.69 us
    dot_general x3, matrix products, project_back(): lax.dot_general(flat_grad, weight, (((1,), (1,)), ((), ())), preferred_el...  4.52 us
  transfers between devices with their start and end apart: 7, of which 3 were waited for; matrix products, arithmetic and copies ran while one was open for 2% of the time, Pallas kernels for 0%

commit v1 on v0

v1 whole, which is shorter than its diff:
```python
import math

import jax
import jax.numpy as jnp
from jax import lax
from jax.experimental import pallas as pl
from jax.experimental.pallas import tpu as pltpu
from jax.sharding import PartitionSpec as P

F32 = jnp.float32
BF16 = jnp.bfloat16
MIB = 1024 * 1024


def column(values):
    size = values.shape[1]
    diagonal = lax.broadcasted_iota(jnp.int32, (size, size), 0) == lax.broadcasted_iota(
        jnp.int32, (size, size), 1
    )
    spread = jnp.where(diagonal, jnp.broadcast_to(values, (size, size)).astype(F32), 0.0)
    return jnp.sum(spread, axis=1, keepdims=True)


def dot(a, b, contract):
    return lax.dot_general(a, b, (contract, ((), ())), preferred_element_type=F32)


def forward(
    chunk,
    inputs_hbm,
    w_query_hbm,
    w_key_hbm,
    w_value_hbm,
    span_ref,
    mode_ref,
    sentinel_ref,
    cotangent_ref,
    denoiser_ref,
    lengths_ref,
    move_ref,
    shaped_hbm,
    inv_ref,
    query_ref,
    key_ref,
    value_ref,
    soft_ref,
    context_ref,
    pay_mate_ref,
    pay_other_ref,
    inputs_v,
    shaped_v,
    w_v,
    in_sem,
    w_sem,
    out_sem,
):
    rows, length, width = inputs_v.shape
    tokens = rows * length
    head = w_v.shape[2]
    chunks = width // chunk
    weights = (w_query_hbm, w_key_hbm, w_value_hbm)

    load = pltpu.make_async_copy(inputs_hbm, inputs_v, in_sem)
    load.start()
    w_loads = []
    for c in range(chunks):
        part = []
        for i, weight in enumerate(weights):
            copy = pltpu.make_async_copy(
                weight.at[pl.ds(c * chunk, chunk)],
                w_v.at[i, pl.ds(c * chunk, chunk)],
                w_sem.at[i, c],
            )
            copy.start()
            part.append(copy)
        w_loads.append(part)

    span = [column(span_ref[r : r + 1, :]) == 1.0 for r in range(rows)]
    load.wait()
    squares = [jnp.zeros((length, 128), F32) for _ in range(rows)]
    for c in range(chunks):
        at = pl.ds(c * chunk, chunk)
        table = mode_ref[:, at].astype(F32)
        sentinel = sentinel_ref[:, at].astype(F32)
        for r in range(rows):
            kind = denoiser_ref[r]
            mode = jnp.where(kind == 0, table[0:1], jnp.where(kind == 1, table[1:2], table[2:3]))
            shaped = jnp.where(span[r], sentinel, inputs_v[r, :, at].astype(F32) + mode)
            shaped = shaped.astype(BF16)
            shaped_v[r * length : (r + 1) * length, at] = shaped
            wide = shaped.astype(F32)
            wide = wide * wide
            for k in range(0, chunk, 128):
                squares[r] = squares[r] + wide[:, k : k + 128]
    store = pltpu.make_async_copy(shaped_v, shaped_hbm, out_sem)
    store.start()
    mean = jnp.concatenate(squares, axis=0)
    mean = jnp.sum(mean, axis=1, keepdims=True) * (1.0 / width)
    inv_rms = lax.rsqrt(mean + 1e-06)
    inv_ref[...] = jnp.broadcast_to(inv_rms, inv_ref.shape)

    totals = [jnp.zeros((tokens, head), F32) for _ in weights]
    for c in range(chunks):
        at = pl.ds(c * chunk, chunk)
        normed = (shaped_v[:, at].astype(F32) * inv_rms).astype(BF16)
        for i in range(len(weights)):
            w_loads[c][i].wait()
            totals[i] = totals[i] + dot(normed, w_v[i, at, :], ((1,), (0,)))
    query, key, value = (total.astype(BF16) for total in totals)
    query_ref[...] = query
    key_ref[...] = key
    value_ref[...] = value

    factor = 1.0 / math.sqrt(head)
    q_at = lax.broadcasted_iota(jnp.int32, (tokens, tokens), 0)
    k_at = lax.broadcasted_iota(jnp.int32, (tokens, tokens), 1)
    ok = jnp.zeros((tokens, tokens), jnp.bool_)
    for r in range(rows):
        low = r * length
        high = low + jnp.maximum(lengths_ref[r], 1)
        ok = ok | (
            (q_at >= low) & (q_at < low + length) & (k_at >= low) & (k_at < high)
        )
    scores = jnp.where(ok, dot(query, key, ((1,), (1,))) * factor, -jnp.inf)
    exp_scores = jnp.exp(scores - jnp.max(scores, axis=1, keepdims=True))
    soft = exp_scores / jnp.sum(exp_scores, axis=1, keepdims=True)
    soft_ref[...] = soft
    context = dot(soft.astype(BF16), value, ((1,), (0,)))
    t_at = lax.broadcasted_iota(jnp.int32, (length, 1), 0)
    mine = []
    for r in range(rows):
        valid = t_at < lengths_ref[r]
        mine.append(jnp.where(valid, context[r * length : (r + 1) * length], 0.0))
    for r in range(rows):
        context_ref[r] = jnp.where(move_ref[r] == 0, mine[r], 0.0).astype(BF16)

    even = lax.rem(lax.axis_index("dp"), 2) == 0
    right = jnp.where(move_ref[0] == 1, mine[0], jnp.where(move_ref[1] == 1, mine[1], 0.0))
    left = jnp.where(move_ref[0] == -1, mine[0], jnp.where(move_ref[1] == -1, mine[1], 0.0))
    right = right.astype(BF16)
    left = left.astype(BF16)

    def pay(ref, to_right):
        ref[0:length, :] = jnp.where(to_right, right, left)
        ref[length : 2 * length, :] = jnp.where(
            to_right, cotangent_ref[rows + 1], cotangent_ref[rows]
        )

    pay(pay_mate_ref, even)
    pay(pay_other_ref, jnp.logical_not(even))
    store.wait()


def backward(
    chunk,
    w_query_hbm,
    w_key_hbm,
    w_value_hbm,
    shaped_hbm,
    inv_ref,
    query_ref,
    key_ref,
    value_ref,
    soft_ref,
    context_ref,
    cotangent_ref,
    got_mate_ref,
    got_other_ref,
    span_ref,
    lengths_ref,
    move_ref,
    out_ref,
    context_out_ref,
    shaped_v,
    w_v,
    grad_v,
    in_sem,
    w_sem,
):
    rows, length, head = context_ref.shape
    tokens, width = shaped_v.shape
    chunks = width // chunk
    weights = (w_query_hbm, w_key_hbm, w_value_hbm)

    w_loads = []
    for c in range(chunks):
        part = []
        for i, weight in enumerate(weights):
            copy = pltpu.make_async_copy(
                weight.at[pl.ds(c * chunk, chunk)],
                w_v.at[i, pl.ds(c * chunk, chunk)],
                w_sem.at[i, c],
            )
            copy.start()
            part.append(copy)
        w_loads.append(part)
        if c == 0:
            load = pltpu.make_async_copy(shaped_hbm, shaped_v, in_sem)
            load.start()

    even = lax.rem(lax.axis_index("dp"), 2) == 0
    got_mate = got_mate_ref[...]
    got_other = got_other_ref[...]
    from_right = jnp.where(even, got_mate, got_other)
    from_left = jnp.where(even, got_other, got_mate)
    for r in range(rows):
        context_out_ref[r] = context_ref[r]
    context_out_ref[rows] = from_left[0:length]
    context_out_ref[rows + 1] = from_right[0:length]

    t_at = lax.broadcasted_iota(jnp.int32, (length, 1), 0)
    grads = []
    for r in range(rows):
        move = move_ref[r]
        grad = jnp.where(
            move == 0,
            cotangent_ref[r],
            jnp.where(move == 1, from_right[length:], from_left[length:]),
        )
        grads.append(jnp.where(t_at < lengths_ref[r], grad.astype(F32), 0.0))
    grad_out = jnp.concatenate(grads, axis=0).astype(BF16)

    factor = 1.0 / math.sqrt(head)
    soft = soft_ref[...]
    grad_value = dot(soft.astype(BF16), grad_out, ((0,), (0,))).astype(BF16)
    grad_soft = dot(grad_out, value_ref[...], ((1,), (1,)))
    row_inner = jnp.sum(soft * grad_soft, axis=1, keepdims=True)
    grad_scores = (soft * (grad_soft - row_inner) * factor).astype(BF16)
    grad_query = dot(grad_scores, key_ref[...], ((1,), (0,))).astype(BF16)
    grad_key = dot(grad_scores, query_ref[...], ((0,), (0,))).astype(BF16)
    gradients = (grad_query, grad_key, grad_value)

    inv_rms = inv_ref[:, 0:1]
    load.wait()
    inner = jnp.zeros((tokens, 128), F32)
    for c in range(chunks):
        at = pl.ds(c * chunk, chunk)
        total = None
        for i in range(len(weights)):
            w_loads[c][i].wait()
            part = dot(gradients[i], w_v[i, at, :], ((1,), (1,)))
            total = part if total is None else total + part
        grad_v[:, at] = total
        product = total * (shaped_v[:, at].astype(F32) * inv_rms)
        for k in range(0, chunk, 128):
            inner = inner + product[:, k : k + 128]
    inner = jnp.sum(inner, axis=1, keepdims=True) * (1.0 / width)

    span = jnp.concatenate([column(span_ref[r : r + 1, :]) for r in range(rows)], axis=0)
    keep = span != 1.0
    pieces, per_row = out_ref.shape[0], out_ref.shape[1] // rows
    for c in range(chunks):
        at = pl.ds(c * chunk, chunk)
        normed = shaped_v[:, at].astype(F32) * inv_rms
        part = (grad_v[:, at] - normed * inner) * inv_rms
        part = jnp.where(keep, part, 0.0)
        for d in range(pieces):
            piece = [
                part[r * length + d * per_row : r * length + (d + 1) * per_row] for r in range(rows)
            ]
            out_ref[d, :, at] = jnp.concatenate(piece, axis=0).astype(BF16)


def exchange(array, pairs):
    return lax.ppermute(array, "dp", pairs)


def shards(
    inputs,
    denoiser,
    span_mask,
    lengths,
    move_plan,
    mode_table,
    sentinel,
    w_query,
    w_key,
    w_value,
    cotangent,
):
    rows, length, width = inputs.shape
    head = w_query.shape[1]
    tokens = rows * length
    groups = lax.axis_size("dp")
    members = lax.axis_size("mp")
    seg = length // members
    chunk = 512
    vmem = pl.BlockSpec(memory_space=pltpu.VMEM)
    smem = pl.BlockSpec(memory_space=pltpu.SMEM)
    hbm = pl.BlockSpec(memory_space=pl.ANY)

    def shape(dims, dtype):
        return jax.ShapeDtypeStruct(dims, dtype)

    shaped, inv_rms, query, key, value, soft, context, pay_mate, pay_other = pl.pallas_call(
        lambda *refs: forward(chunk, *refs),
        out_shape=(
            shape((tokens, width), BF16),
            shape((tokens, 128), F32),
            shape((tokens, head), BF16),
            shape((tokens, head), BF16),
            shape((tokens, head), BF16),
            shape((tokens, tokens), F32),
            shape((rows, length, head), BF16),
            shape((2 * length, head), BF16),
            shape((2 * length, head), BF16),
        ),
        in_specs=[hbm] * 4 + [vmem] * 4 + [smem] * 3,
        out_specs=[hbm] + [vmem] * 8,
        scratch_shapes=[
            pltpu.VMEM((rows, length, width), BF16),
            pltpu.VMEM((tokens, width), BF16),
            pltpu.VMEM((3, width, head), BF16),
            pltpu.SemaphoreType.DMA,
            pltpu.SemaphoreType.DMA((3, width // chunk)),
            pltpu.SemaphoreType.DMA,
        ],
        compiler_params=pltpu.CompilerParams(vmem_limit_bytes=40 * MIB),
        name="forward",
    )(
        inputs,
        w_query,
        w_key,
        w_value,
        span_mask,
        mode_table,
        sentinel.reshape(1, width),
        cotangent,
        denoiser,
        lengths,
        move_plan,
    )

    others = [(g, (g + 1) % groups if g % 2 else (g - 1) % groups) for g in range(groups)]
    got_other = exchange(pay_other, others)
    got_mate = exchange(pay_mate, [(g, g ^ 1) for g in range(groups)])

    head_part, context = pl.pallas_call(
        lambda *refs: backward(chunk, *refs),
        out_shape=(
            shape((members, rows * seg, width), BF16),
            shape((2 * rows, length, head), BF16),
        ),
        in_specs=[hbm] * 4 + [vmem] * 10 + [smem] * 2,
        out_specs=[vmem, vmem],
        scratch_shapes=[
            pltpu.VMEM((tokens, width), BF16),
            pltpu.VMEM((3, width, head), BF16),
            pltpu.VMEM((tokens, width), F32),
            pltpu.SemaphoreType.DMA,
            pltpu.SemaphoreType.DMA((3, width // chunk)),
        ],
        compiler_params=pltpu.CompilerParams(vmem_limit_bytes=40 * MIB),
        name="backward",
    )(
        w_query,
        w_key,
        w_value,
        shaped,
        inv_rms,
        query,
        key,
        value,
        soft,
        context,
        cotangent,
        got_mate,
        got_other,
        span_mask,
        lengths,
        move_plan,
    )
    summed = lax.psum_scatter(head_part, "mp", scatter_dimension=0)
    return (context, summed.reshape(rows, seg, width))


def solution(mesh):
    return jax.shard_map(
        shards,
        mesh=mesh,
        in_specs=(
            P("dp", None, None),
            P("dp"),
            P("dp", None),
            P("dp"),
            P("dp"),
            P(),
            P(),
            P(None, "mp"),
            P(None, "mp"),
            P(None, "mp"),
            P("dp", None, "mp"),
        ),
        out_specs=(P("dp", None, "mp"), P("dp", "mp", None)),
        check_vma=False,
    )
```

time: 203 us -> 112 us (0.55)
  waiting for transfers between devices: 129 us -> 67.2 us
  other arithmetic: 19.7 us -> 0 us
  starting transfers between devices: 19.6 us -> 5.32 us
  Pallas kernels: 0 us -> 11.5 us
  matrix products: 8.37 us -> 0 us
  local copies, waits for them, and re-layouts: 6.32 us -> 12.4 us
  between operations: 18.6 us -> 14.1 us
    unnamed x2 -> x1, waiting for transfers between devices: 123 us -> 0.02 us
    reduce_scatter x0 -> x1, waiting for transfers between devices: none -> 65.1 us  [shards(): summed = lax.psum_scatter(head_part, 'mp', scatter_dimension=0)]
    ppermute x6 -> x2, starting transfers between devices: 19.5 us -> 5.28 us  [exchange(): return lax.ppermute(array, 'dp', pairs)]
    pallas_call x0 -> x2, Pallas kernels: none -> 11.5 us  [the longest x1 6.48 us: shards(): pl.pallas_call(lambda *refs: backward(chunk, *refs), out_shape=(shape((me...]
    dot_general x12 -> x0, matrix products: 8.37 us -> none  [the longest x3 4.52 us: project_back(): lax.dot_general(flat_grad, weight, (((1,), (1,)), ((), ())), preferred_el...]
    convert_element_type x5 -> x0, other arithmetic: 5.59 us -> none  [the longest x1 1.91 us: attend(): slot_rows.astype(jnp.float32).reshape(slot_count * length, model_width)]
    select_n x3 -> x0, other arithmetic: 4.1 us -> none  [the longest x1 1.62 us: shards(): jnp.where((span_piece == 1)[:, :, None], jnp.zeros_like(summed), summed)]
    unnamed x23 -> x28, local copies, waits for them, and re-layouts: 6.13 us -> 10.2 us
  transfers between devices with their start and end apart: 7 -> 3, of which waited for: 3 -> 2; matrix products, arithmetic and copies ran while one was open for 2% -> 0% of each run, Pallas kernels for 0% -> 0%
where the time goes in v1:
time: 112 us; the launch traced here: 111 us
  waiting for transfers between devices  67.2 us (60%)
  between operations  14.1 us (13%)
  local copies, waits for them, and re-layouts  12.4 us (11%)
  Pallas kernels  11.5 us (10%)
  starting transfers between devices  5.32 us (5%)
    reduce_scatter x1, waiting for transfers between devices, shards(): summed = lax.psum_scatter(head_part, 'mp', scatter_dimension=0)  65.1 us
    unnamed x28, local copies, waits for them, and re-layouts  10.2 us
    pallas_call x1, Pallas kernels, shards(): pl.pallas_call(lambda *refs: backward(chunk, *refs), out_shape=(shape((me...  6.48 us
    ppermute x2, starting transfers between devices, exchange(): return lax.ppermute(array, 'dp', pairs)  5.28 us
    pallas_call x1, Pallas kernels, shards(): pl.pallas_call(lambda *refs: forward(chunk, *refs), out_shape=(shape((tok...  5 us
  transfers between devices with their start and end apart: 3, of which 2 were waited for; matrix products, arithmetic and copies ran while one was open for 0% of the time, Pallas kernels for 0%

profile of v1, /device:TPU:56, one launch (start us, length us, event | category | flops | bytes accessed | tf_op | source)
XLA Modules:
  0.0 110.5 jit_solution(14506004895165818894)
XLA Ops:
  7.2 0.0 reduce-scatter.2.cloned.1.call-start
  7.2 0.7 reshape.7.refs_6_
  7.9 0.0 copy-start
  7.9 1.6 %copy-done = bf16[4096,256]{1,0:T(8,128)(2,1)S(1)} copy-done((bf16[4096,256]{1,0:T(8,128)(2,1)S(1)}, bf16[4096,256]{1,0:T(8,128)(2,1)}, u32[]{:S(2)}) %copy-start) | copy-done | bytes 2097176
  9.5 0.0 copy-start.2
  9.5 1.6 %copy-done.2 = bf16[4096,256]{1,0:T(8,128)(2,1)S(1)} copy-done((bf16[4096,256]{1,0:T(8,128)(2,1)S(1)}, bf16[4096,256]{1,0:T(8,128)(2,1)}, u32[]{:S(2)}) %copy-start.2) | copy-done | bytes 2097176
  11.1 0.0 copy-start.4
  11.1 1.6 %copy-done.4 = bf16[4096,256]{1,0:T(8,128)(2,1)S(1)} copy-done((bf16[4096,256]{1,0:T(8,128)(2,1)S(1)}, bf16[4096,256]{1,0:T(8,128)(2,1)}, u32[]{:S(2)}) %copy-start.4) | copy-done | bytes 2097176
  12.7 0.0 copy-start.6
  12.7 1.1 %copy-done.6 = bf16[2,48,4096]{2,1,0:T(8,128)(2,1)S(1)} copy-done((bf16[2,48,4096]{2,1,0:T(8,128)(2,1)S(1)}, bf16[2,48,4096]{2,1,0:T(8,128)(2,1)}, u32[]{:S(2)}) %copy-start.6) | copy-done | bytes 786456
  13.8 0.0 copy-start.7
  13.8 0.9 copy-done.7
  14.7 0.0 copy-start.9
  14.7 0.8 copy-done.9
  15.5 0.0 copy-start.10
  15.5 0.7 copy-done.10
  16.2 0.7 copy-done.11
  16.8 0.7 copy-done.12
  17.5 0.7 copy-done.13
  18.1 5.0 %forward.1 = (bf16[96,4096]{1,0:T(8,128)(2,1)S(1)}, f32[96,128]{1,0:T(8,128)S(1)}, bf16[96,256]{1,0:T(8,128)(2,1)S(1)}, bf16[96,256]{1,0:T(8,128)(2,1)S(1)}, bf1...) custom-call(bf16[2,48,4096]{2,1,0:T(8,128)(2,1)S(1)} %copy-done.6, ...), custom_call_target="tpu_custom_call" | custom-call | tf_op jit(solution)/shard_map/forward/pallas_call | solution.py:295
  23.1 1.9 %collective-permute-start = (bf16[96,256]{1,0:T(8,128)(2,1)S(1)}, bf16[96,256]{1,0:T(8,128)(2,1)S(1)}, u32[]{:S(2)}, u32[]{:S(2)}) collective-permute-start(bf16[96,256]{1,0:T(8,128)(2,1)S(1)} %get-tuple-element.20), channel_id=1, source_target_pairs={{0,12},{12,0},{24,36},{36,24},{48,60},{60,48},{72,84},{84,72},{96,... | collective-permute-start | bytes 147464 | tf_op jit(solution)/shard_map/ppermute | solution.py:265
  25.1 3.4 %collective-permute-start.1 = (bf16[96,256]{1,0:T(8,128)(2,1)S(1)}, bf16[96,256]{1,0:T(8,128)(2,1)S(1)}, u32[]{:S(2)}, u32[]{:S(2)}) collective-permute-start(bf16[96,256]{1,0:T(8,128)(2,1)S(1)} %get-tuple-element.21), channel_id=1, source_target_pairs={{0,756},{12,24},{24,12},{36,48},{48,36},{60,72},{72,60},{84,96},{9... | collective-permute-start | bytes 147464 | tf_op jit(solution)/shard_map/ppermute | solution.py:265
  28.4 0.0 collective-permute-done.refs_11_
  28.5 2.0 %collective-permute-done.1.refs_12_ = bf16[96,256]{1,0:T(8,128)(2,1)S(1)} collective-permute-done((bf16[96,256]{1,0:T(8,128)(2,1)S(1)}, bf16[96,256]{1,0:T(8,128)(2,1)S(1)}, u32[]{:S(2)}, u32[]{:S(2)}) %collective-permute-start.1) | collective-permute-done | bytes 49184 | tf_op jit(solution)/shard_map/ppermute | solution.py:265
  30.5 0.0 copy-done.1
  30.5 0.0 copy-done.3
  30.5 0.0 copy-done.5
  30.5 0.0 copy-done.8
  30.5 6.5 %backward.1 = (bf16[12,8,4096]{2,1,0:T(8,128)(2,1)}, bf16[4,48,256]{2,1,0:T(8,128)(2,1)}) custom-call(bf16[4096,256]{1,0:T(8,128)(2,1)S(1)} %copy-done.1, bf16[4096,256]{1,0:T(8,128)(2,1)S(1)} %copy-done.3, bf16[4096,256]{1,0:T(8,128)(2,1)S(1)} %copy-done.5, bf16[96,4096]{1,0:T(8,128)(2,1)S(1)} %get-tuple-element.13.refs_3_, ...), custom_call_target="tpu_custom_call" | custom-call | tf_op jit(solution)/shard_map/backward/pallas_call | solution.py:338
  37.0 0.0 reduce-scatter.2.cloned.1.call-update
  37.0 65.1 %reduce-scatter.2.cloned.1.call-done = bf16[1,8,4096]{2,1,0:T(8,128)(2,1)} async-done(((bf16[12,8,4096]{2,1,0:T(8,128)(2,1)}), bf16[1,8,4096]{2,1,0:T(8,128)(2,1)}) %reduce-scatter.2.cloned.1.call-update) | async-done | bytes 65552 | tf_op jit(solution)/shard_map/reduce_scatter | solution.py:373
  102.2 1.5 %reshape_reduce_scatter.3 = bf16[2,4,4096]{2,1,0:T(4,128)(2,1)} reshape(bf16[1,8,4096]{2,1,0:T(8,128)(2,1)} %reduce-scatter.2.cloned.1.call-done) | data formatting | bytes 131072 | tf_op jit(solution)/shard_map/reshape;reduce_scatter | solution.py:374
  (7 shorter events, 0.0 us)
Async XLA Ops:
  7.2 95.0 %reduce-scatter.2.cloned.1.call-start = ((), (), s32[]{:S(2)}) async-start(), calls=%async_computation.1 | async-start | bytes 851968 | tf_op jit(solution)/shard_map/reduce_scatter | solution.py:373
  7.9 1.6 %copy-start = (bf16[4096,256]{1,0:T(8,128)(2,1)S(1)}, bf16[4096,256]{1,0:T(8,128)(2,1)}, u32[]{:S(2)}) copy-start(bf16[4096,256]{1,0:T(8,128)(2,1)} %refs_0_.3) | copy-start | bytes 6291460
  9.5 1.6 %copy-start.2 = (bf16[4096,256]{1,0:T(8,128)(2,1)S(1)}, bf16[4096,256]{1,0:T(8,128)(2,1)}, u32[]{:S(2)}) copy-start(bf16[4096,256]{1,0:T(8,128)(2,1)} %refs_1_.3) | copy-start | bytes 6291460
  11.1 1.6 %copy-start.4 = (bf16[4096,256]{1,0:T(8,128)(2,1)S(1)}, bf16[4096,256]{1,0:T(8,128)(2,1)}, u32[]{:S(2)}) copy-start(bf16[4096,256]{1,0:T(8,128)(2,1)} %refs_2_.3) | copy-start | bytes 6291460
  12.7 1.1 %copy-start.6 = (bf16[2,48,4096]{2,1,0:T(8,128)(2,1)S(1)}, bf16[2,48,4096]{2,1,0:T(8,128)(2,1)}, u32[]{:S(2)}) copy-start(bf16[2,48,4096]{2,1,0:T(8,128)(2,1)} %refs_0_.2) | copy-start | bytes 2359300
  13.8 0.9 copy-start.7
  14.7 0.8 copy-start.9
  15.5 0.7 copy-start.10
  16.2 0.7 copy-start.11
  16.8 0.7 copy-start.12
  17.5 0.7 copy-start.13
  18.1 12.4 %copy-start.1 = (bf16[4096,256]{1,0:T(8,128)(2,1)S(1)}, bf16[4096,256]{1,0:T(8,128)(2,1)}, u32[]{:S(2)}) copy-start(bf16[4096,256]{1,0:T(8,128)(2,1)} %refs_0_.3) | copy-start | bytes 6291460
  18.1 12.4 %copy-start.3 = (bf16[4096,256]{1,0:T(8,128)(2,1)S(1)}, bf16[4096,256]{1,0:T(8,128)(2,1)}, u32[]{:S(2)}) copy-start(bf16[4096,256]{1,0:T(8,128)(2,1)} %refs_1_.3) | copy-start | bytes 6291460
  18.1 12.4 %copy-start.5 = (bf16[4096,256]{1,0:T(8,128)(2,1)S(1)}, bf16[4096,256]{1,0:T(8,128)(2,1)}, u32[]{:S(2)}) copy-start(bf16[4096,256]{1,0:T(8,128)(2,1)} %refs_2_.3) | copy-start | bytes 6291460
  18.1 12.4 %copy-start.8 = (bf16[4,48,256]{2,1,0:T(8,128)(2,1)S(1)}, bf16[4,48,256]{2,1,0:T(8,128)(2,1)}, u32[]{:S(2)}) copy-start(bf16[4,48,256]{2,1,0:T(8,128)(2,1)} %refs_10_.3) | copy-start | bytes 294916
  23.1 5.3 %collective-permute-start = (bf16[96,256]{1,0:T(8,128)(2,1)S(1)}, bf16[96,256]{1,0:T(8,128)(2,1)S(1)}, u32[]{:S(2)}, u32[]{:S(2)}) collective-permute-start(bf16[96,256]{1,0:T(8,128)(2,1)S(1)} %get-tuple-element.20), channel_id=1, source_target_pairs={{0,12},{12,0},{24,36},{36,24},{48,60},{60,48},{72,84},{84,72},{96,... | collective-permute-start | bytes 147464 | tf_op jit(solution)/shard_map/ppermute | solution.py:265
  25.1 5.4 %collective-permute-start.1 = (bf16[96,256]{1,0:T(8,128)(2,1)S(1)}, bf16[96,256]{1,0:T(8,128)(2,1)S(1)}, u32[]{:S(2)}, u32[]{:S(2)}) collective-permute-start(bf16[96,256]{1,0:T(8,128)(2,1)S(1)} %get-tuple-element.21), channel_id=1, source_target_pairs={{0,756},{12,24},{24,12},{36,48},{48,36},{60,72},{72,60},{84,96},{9... | collective-permute-start | bytes 147464 | tf_op jit(solution)/shard_map/ppermute | solution.py:265
Sparse Core Ops, SparseCore 0:
  37.1 64.9 reduce-scatter.1

commit v2 on v1

v2 whole, which is shorter than its diff:
```python
import math

import jax
import jax.numpy as jnp
from jax import lax
from jax.experimental import pallas as pl
from jax.experimental.pallas import tpu as pltpu
from jax.sharding import PartitionSpec as P

F32 = jnp.float32
BF16 = jnp.bfloat16
MIB = 1024 * 1024


def column(values):
    size = values.shape[1]
    diagonal = lax.broadcasted_iota(jnp.int32, (size, size), 0) == lax.broadcasted_iota(
        jnp.int32, (size, size), 1
    )
    spread = jnp.where(diagonal, jnp.broadcast_to(values, (size, size)).astype(F32), 0.0)
    return jnp.sum(spread, axis=1, keepdims=True)


def dot(a, b, contract):
    return lax.dot_general(a, b, (contract, ((), ())), preferred_element_type=F32)


def forward(
    chunk,
    inputs_hbm,
    denoiser_hbm,
    span_hbm,
    lengths_hbm,
    move_hbm,
    mode_hbm,
    sentinel_hbm,
    w_query_hbm,
    w_key_hbm,
    w_value_hbm,
    cotangent_hbm,
    shaped_ref,
    w_ref,
    marks_ref,
    query_ref,
    key_ref,
    value_ref,
    soft_ref,
    context_ref,
    own_ref,
    pay_mate_ref,
    pay_other_ref,
    inputs_v,
    span_v,
    mode_v,
    sentinel_v,
    cotangent_v,
    denoiser_s,
    lengths_s,
    move_s,
    sem,
    w_sem,
):
    rows, length, width = inputs_v.shape
    tokens = rows * length
    head = w_ref.shape[2]
    chunks = width // chunk
    weights = (w_query_hbm, w_key_hbm, w_value_hbm)

    small = [
        pltpu.make_async_copy(source, target, sem.at[i])
        for i, (source, target) in enumerate(
            (
                (denoiser_hbm, denoiser_s),
                (span_hbm, span_v),
                (mode_hbm, mode_v),
                (sentinel_hbm, sentinel_v),
                (inputs_hbm, inputs_v),
                (lengths_hbm, lengths_s),
                (move_hbm, move_s),
                (cotangent_hbm, cotangent_v),
            )
        )
    ]
    for copy in small[:5]:
        copy.start()
    w_loads = []
    for c in range(chunks):
        part = []
        for i, weight in enumerate(weights):
            copy = pltpu.make_async_copy(
                weight.at[pl.ds(c * chunk, chunk)],
                w_ref.at[i, pl.ds(c * chunk, chunk)],
                w_sem.at[i, c],
            )
            copy.start()
            part.append(copy)
        w_loads.append(part)
    for copy in small[5:]:
        copy.start()

    for copy in small[:5]:
        copy.wait()
    span = [column(span_v[r : r + 1, :]) == 1.0 for r in range(rows)]
    squares = [jnp.zeros((length, 128), F32) for _ in range(rows)]
    for c in range(chunks):
        at = pl.ds(c * chunk, chunk)
        table = mode_v[:, at].astype(F32)
        sentinel = sentinel_v[at].astype(F32).reshape(1, chunk)
        for r in range(rows):
            kind = denoiser_s[r]
            mode = jnp.where(kind == 0, table[0:1], jnp.where(kind == 1, table[1:2], table[2:3]))
            shaped = jnp.where(span[r], sentinel, inputs_v[r, :, at].astype(F32) + mode)
            shaped = shaped.astype(BF16)
            shaped_ref[r * length : (r + 1) * length, at] = shaped
            wide = shaped.astype(F32)
            wide = wide * wide
            for k in range(0, chunk, 128):
                squares[r] = squares[r] + wide[:, k : k + 128]
    mean = jnp.concatenate(squares, axis=0)
    mean = jnp.sum(mean, axis=1, keepdims=True) * (1.0 / width)
    inv_rms = lax.rsqrt(mean + 1e-06)

    totals = [jnp.zeros((tokens, head), F32) for _ in weights]
    for c in range(chunks):
        at = pl.ds(c * chunk, chunk)
        normed = (shaped_ref[:, at].astype(F32) * inv_rms).astype(BF16)
        for i in range(len(weights)):
            w_loads[c][i].wait()
            totals[i] = totals[i] + dot(normed, w_ref[i, at, :], ((1,), (0,)))
    query, key, value = (total.astype(BF16) for total in totals)
    query_ref[...] = query
    key_ref[...] = key
    value_ref[...] = value

    for copy in small[5:]:
        copy.wait()
    factor = 1.0 / math.sqrt(head)
    q_at = lax.broadcasted_iota(jnp.int32, (tokens, tokens), 0)
    k_at = lax.broadcasted_iota(jnp.int32, (tokens, tokens), 1)
    ok = jnp.zeros((tokens, tokens), jnp.bool_)
    for r in range(rows):
        low = r * length
        high = low + jnp.maximum(lengths_s[r], 1)
        ok = ok | ((q_at >= low) & (q_at < low + length) & (k_at >= low) & (k_at < high))
    scores = jnp.where(ok, dot(query, key, ((1,), (1,))) * factor, -jnp.inf)
    exp_scores = jnp.exp(scores - jnp.max(scores, axis=1, keepdims=True))
    soft = exp_scores / jnp.sum(exp_scores, axis=1, keepdims=True)
    soft_ref[...] = soft
    context = dot(soft.astype(BF16), value, ((1,), (0,)))

    t_at = lax.broadcasted_iota(jnp.int32, (length, 128), 0)
    lane = lax.broadcasted_iota(jnp.int32, (length, 128), 1)
    mine = []
    for r in range(rows):
        move = move_s[r]
        valid = t_at < lengths_s[r]
        here = slice(r * length, (r + 1) * length)
        mine.append(jnp.where(valid[:, 0:1], context[here], 0.0))
        own = jnp.where(valid[:, 0:1], cotangent_v[r].astype(F32), 0.0)
        own_ref[here, :] = jnp.where(move == 0, own, 0.0).astype(BF16)
        context_ref[r] = jnp.where(move == 0, mine[r], 0.0).astype(BF16)
        marks = jnp.where(lane == 0, inv_rms[here], 0.0)
        marks = jnp.where((lane == 1) & valid & (move == 1), 1.0, marks)
        marks = jnp.where((lane == 2) & valid & (move == -1), 1.0, marks)
        marks_ref[here, :] = jnp.where((lane == 3) & jnp.logical_not(span[r]), 1.0, marks)

    even = lax.rem(lax.axis_index("dp"), 2) == 0
    right = jnp.where(move_s[0] == 1, mine[0], jnp.where(move_s[1] == 1, mine[1], 0.0))
    left = jnp.where(move_s[0] == -1, mine[0], jnp.where(move_s[1] == -1, mine[1], 0.0))
    right = right.astype(BF16)
    left = left.astype(BF16)

    def pay(ref, to_right):
        ref[0:length, :] = jnp.where(to_right, right, left)
        ref[length : 2 * length, :] = jnp.where(
            to_right, cotangent_v[rows + 1], cotangent_v[rows]
        )

    pay(pay_mate_ref, even)
    pay(pay_other_ref, jnp.logical_not(even))


def backward(
    chunk,
    shaped_ref,
    w_ref,
    marks_ref,
    query_ref,
    key_ref,
    value_ref,
    soft_ref,
    context_ref,
    own_ref,
    got_mate_ref,
    got_other_ref,
    out_ref,
    context_out_ref,
    grad_v,
):
    rows, length, head = context_ref.shape
    tokens, width = shaped_ref.shape
    chunks = width // chunk

    even = lax.rem(lax.axis_index("dp"), 2) == 0
    got_mate = got_mate_ref[...]
    got_other = got_other_ref[...]
    from_right = jnp.where(even, got_mate, got_other)
    from_left = jnp.where(even, got_other, got_mate)
    for r in range(rows):
        context_out_ref[r] = context_ref[r]
    context_out_ref[rows] = from_left[0:length]
    context_out_ref[rows + 1] = from_right[0:length]

    marks = marks_ref[...]
    inv_rms = marks[:, 0:1]
    right_grad = from_right[length:].astype(F32)
    left_grad = from_left[length:].astype(F32)
    right_grad = jnp.concatenate([right_grad] * rows, axis=0)
    left_grad = jnp.concatenate([left_grad] * rows, axis=0)
    grad_out = jnp.where(
        marks[:, 1:2] == 1.0,
        right_grad,
        jnp.where(marks[:, 2:3] == 1.0, left_grad, own_ref[...].astype(F32)),
    ).astype(BF16)

    factor = 1.0 / math.sqrt(head)
    soft = soft_ref[...]
    grad_value = dot(soft.astype(BF16), grad_out, ((0,), (0,))).astype(BF16)
    grad_soft = dot(grad_out, value_ref[...], ((1,), (1,)))
    row_inner = jnp.sum(soft * grad_soft, axis=1, keepdims=True)
    grad_scores = (soft * (grad_soft - row_inner) * factor).astype(BF16)
    grad_query = dot(grad_scores, key_ref[...], ((1,), (0,))).astype(BF16)
    grad_key = dot(grad_scores, query_ref[...], ((0,), (0,))).astype(BF16)
    gradients = (grad_query, grad_key, grad_value)

    inner = jnp.zeros((tokens, 128), F32)
    for c in range(chunks):
        at = pl.ds(c * chunk, chunk)
        total = None
        for i in range(3):
            part = dot(gradients[i], w_ref[i, at, :], ((1,), (1,)))
            total = part if total is None else total + part
        grad_v[:, at] = total
        product = total * (shaped_ref[:, at].astype(F32) * inv_rms)
        for k in range(0, chunk, 128):
            inner = inner + product[:, k : k + 128]
    inner = jnp.sum(inner, axis=1, keepdims=True) * (1.0 / width)

    keep = marks[:, 3:4] == 1.0
    pieces, _, per_row, _ = out_ref.shape
    for c in range(chunks):
        at = pl.ds(c * chunk, chunk)
        normed = shaped_ref[:, at].astype(F32) * inv_rms
        part = (grad_v[:, at] - normed * inner) * inv_rms
        part = jnp.where(keep, part, 0.0).astype(BF16)
        for d in range(pieces):
            for r in range(rows):
                first = r * length + d * per_row
                out_ref[d, r, :, at] = part[first : first + per_row]


def exchange(array, pairs):
    return lax.ppermute(array, "dp", pairs)


def shards(
    inputs,
    denoiser,
    span_mask,
    lengths,
    move_plan,
    mode_table,
    sentinel,
    w_query,
    w_key,
    w_value,
    cotangent,
):
    rows, length, width = inputs.shape
    head = w_query.shape[1]
    tokens = rows * length
    groups = lax.axis_size("dp")
    members = lax.axis_size("mp")
    seg = length // members
    chunk = 512
    vmem = pl.BlockSpec(memory_space=pltpu.VMEM)
    hbm = pl.BlockSpec(memory_space=pltpu.HBM)

    def shape(dims, dtype):
        return jax.ShapeDtypeStruct(dims, dtype)

    *kept, pay_mate, pay_other = pl.pallas_call(
        lambda *refs: forward(chunk, *refs),
        out_shape=(
            shape((tokens, width), BF16),
            shape((3, width, head), BF16),
            shape((tokens, 128), F32),
            shape((tokens, head), BF16),
            shape((tokens, head), BF16),
            shape((tokens, head), BF16),
            shape((tokens, tokens), F32),
            shape((rows, length, head), BF16),
            shape((tokens, head), BF16),
            shape((2 * length, head), BF16),
            shape((2 * length, head), BF16),
        ),
        in_specs=[hbm] * 11,
        out_specs=[vmem] * 11,
        scratch_shapes=[
            pltpu.VMEM((rows, length, width), BF16),
            pltpu.VMEM(span_mask.shape, jnp.int32),
            pltpu.VMEM(mode_table.shape, BF16),
            pltpu.VMEM((width,), BF16),
            pltpu.VMEM(cotangent.shape, BF16),
            pltpu.SMEM((rows,), jnp.int32),
            pltpu.SMEM((rows,), jnp.int32),
            pltpu.SMEM((rows,), jnp.int32),
            pltpu.SemaphoreType.DMA((8,)),
            pltpu.SemaphoreType.DMA((3, width // chunk)),
        ],
        compiler_params=pltpu.CompilerParams(vmem_limit_bytes=24 * MIB),
        name="forward",
    )(
        *(
            pltpu.with_memory_space_constraint(array, pltpu.HBM)
            for array in (
                inputs,
                denoiser,
                span_mask,
                lengths,
                move_plan,
                mode_table,
                sentinel,
                w_query,
                w_key,
                w_value,
                cotangent,
            )
        )
    )

    others = [(g, (g + 1) % groups if g % 2 else (g - 1) % groups) for g in range(groups)]
    got_other = exchange(pay_other, others)
    got_mate = exchange(pay_mate, [(g, g ^ 1) for g in range(groups)])

    head_part, context = pl.pallas_call(
        lambda *refs: backward(chunk, *refs),
        out_shape=(
            shape((members, rows, seg, width), BF16),
            shape((2 * rows, length, head), BF16),
        ),
        in_specs=[vmem] * 11,
        out_specs=[vmem, vmem],
        scratch_shapes=[pltpu.VMEM((tokens, width), F32)],
        compiler_params=pltpu.CompilerParams(vmem_limit_bytes=24 * MIB),
        name="backward",
    )(*kept, got_mate, got_other)
    heads = lax.all_to_all(head_part, "mp", 0, 0)
    return (context, jnp.sum(heads.astype(F32), axis=0).astype(BF16))


def solution(mesh):
    return jax.shard_map(
        shards,
        mesh=mesh,
        in_specs=(
            P("dp", None, None),
            P("dp"),
            P("dp", None),
            P("dp"),
            P("dp"),
            P(),
            P(),
            P(None, "mp"),
            P(None, "mp"),
            P(None, "mp"),
            P("dp", None, "mp"),
        ),
        out_specs=(P("dp", None, "mp"), P("dp", "mp", None)),
        check_vma=False,
    )
```

time: 112 us -> 68.4 us (0.61)
  the two profiles are of different devices: /device:TPU:56 before, /device:TPU:63 now
where the time goes in v2:
time: 68.4 us; the launch traced here: 68.2 us
  blocking collectives  41.7 us (61%)
  starting transfers between devices  12.8 us (19%)
  Pallas kernels  10.3 us (15%)
  waiting for transfers between devices  1.75 us (3%)
  other arithmetic  0.98 us (1%)
    all_to_all x1, blocking collectives, shards(): heads = lax.all_to_all(head_part, 'mp', 0, 0)  41.7 us
    ppermute x2, starting transfers between devices, exchange(): return lax.ppermute(array, 'dp', pairs)  12.8 us
    pallas_call x1, Pallas kernels, shards(): pl.pallas_call(lambda *refs: forward(chunk, *refs), out_shape=(shape((tok...  6.79 us
    pallas_call x1, Pallas kernels, shards(): pl.pallas_call(lambda *refs: backward(chunk, *refs), out_shape=(shape((me...  3.51 us
    ppermute x2, waiting for transfers between devices, exchange(): return lax.ppermute(array, 'dp', pairs)  1.75 us
  transfers between devices with their start and end apart: 2, of which 1 were waited for; matrix products, arithmetic and copies ran while one was open for 0% of the time, Pallas kernels for 0%

profile of v2, /device:TPU:63, one launch (start us, length us, event | category | flops | bytes accessed | tf_op | source)
XLA Modules:
  0.0 68.2 jit_solution(3394599112529870625)
XLA Ops:
  0.6 6.8 %forward.1 = (bf16[96,4096]{1,0:T(8,128)(2,1)S(1)}, bf16[3,4096,256]{2,1,0:T(8,128)(2,1)S(1)}, f32[96,128]{1,0:T(8,128)S(1)}, bf16[96,256]{1,0:T(8,128)(2,1)S(1)...) custom-call(bf16[2,48,4096]{2,1,0:T(8,128)(2,1)} %refs_0_.1, ...), custom_call_target="tpu_custom_call" | custom-call | tf_op jit(solution)/shard_map/forward/pallas_call | solution.py:292
  7.4 2.6 %collective-permute-start = (bf16[96,256]{1,0:T(8,128)(2,1)S(1)}, bf16[96,256]{1,0:T(8,128)(2,1)S(1)}, u32[]{:S(2)}, u32[]{:S(2)}) collective-permute-start(bf16[96,256]{1,0:T(8,128)(2,1)S(1)} %get-tuple-element.24), channel_id=1, source_target_pairs={{0,12},{12,0},{24,36},{36,24},{48,60},{60,48},{72,84},{84,72},{96,... | collective-permute-start | bytes 147464 | tf_op jit(solution)/shard_map/ppermute | solution.py:263
  10.0 10.2 %collective-permute-start.1 = (bf16[96,256]{1,0:T(8,128)(2,1)S(1)}, bf16[96,256]{1,0:T(8,128)(2,1)S(1)}, u32[]{:S(2)}, u32[]{:S(2)}) collective-permute-start(bf16[96,256]{1,0:T(8,128)(2,1)S(1)} %get-tuple-element.25), channel_id=1, source_target_pairs={{0,756},{12,24},{24,12},{36,48},{48,36},{60,72},{72,60},{84,96},{9... | collective-permute-start | bytes 147464 | tf_op jit(solution)/shard_map/ppermute | solution.py:263
  20.3 0.0 collective-permute-done.refs_9_
  20.3 1.7 %collective-permute-done.1.refs_10_ = bf16[96,256]{1,0:T(8,128)(2,1)S(1)} collective-permute-done((bf16[96,256]{1,0:T(8,128)(2,1)S(1)}, bf16[96,256]{1,0:T(8,128)(2,1)S(1)}, u32[]{:S(2)}, u32[]{:S(2)}) %collective-permute-start.1) | collective-permute-done | bytes 49184 | tf_op jit(solution)/shard_map/ppermute | solution.py:263
  22.0 3.5 %backward.1 = (bf16[12,2,4,4096]{3,2,1,0:T(4,128)(2,1)S(1)}, bf16[4,48,256]{2,1,0:T(8,128)(2,1)}) custom-call(bf16[96,4096]{1,0:T(8,128)(2,1)S(1)} %get-tuple-element.15.refs_0_, bf16[3,4096,256]{2,1,0:T(8,128)(2,1)S(1)} %get-tuple-element.16.refs_1_, f32[96,128]{1,0:T(8,128)S(1)} %get-tuple-element.17.refs_2_, ...), custom_call_target="tpu_custom_call" | custom-call | tf_op jit(solution)/shard_map/backward/pallas_call | solution.py:346
  25.5 41.7 %all_to_all.5 = bf16[12,2,4,4096]{3,2,1,0:T(4,128)(2,1)S(1)} all-to-all(bf16[12,2,4,4096]{3,2,1,0:T(4,128)(2,1)S(1)} %get-tuple-element.27), channel_id=1, replica_groups=mesh['dp'=64,'mp'=12] {'mp'}, dimensions={0} | all-to-all | bytes 1572864 | tf_op jit(solution)/shard_map/all_to_all | solution.py:358
  67.2 1.0 %reduce_sum.12 = bf16[2,4,4096]{2,1,0:T(4,128)(2,1)} reduce(bf16[12,2,4,4096]{3,2,1,0:T(4,128)(2,1)S(1)} %all_to_all.5, bf16[]{:T(256)} %constant.2.clone.1), dimensions={0}, to_apply=%region_0.0 | reduce | flops 360448 | bytes 851970 | tf_op jit(solution)/shard_map/reduce_sum | solution.py:359
Async XLA Ops:
  7.4 12.8 %collective-permute-start = (bf16[96,256]{1,0:T(8,128)(2,1)S(1)}, bf16[96,256]{1,0:T(8,128)(2,1)S(1)}, u32[]{:S(2)}, u32[]{:S(2)}) collective-permute-start(bf16[96,256]{1,0:T(8,128)(2,1)S(1)} %get-tuple-element.24), channel_id=1, source_target_pairs={{0,12},{12,0},{24,36},{36,24},{48,60},{60,48},{72,84},{84,72},{96,... | collective-permute-start | bytes 147464 | tf_op jit(solution)/shard_map/ppermute | solution.py:263
  10.0 12.0 %collective-permute-start.1 = (bf16[96,256]{1,0:T(8,128)(2,1)S(1)}, bf16[96,256]{1,0:T(8,128)(2,1)S(1)}, u32[]{:S(2)}, u32[]{:S(2)}) collective-permute-start(bf16[96,256]{1,0:T(8,128)(2,1)S(1)} %get-tuple-element.25), channel_id=1, source_target_pairs={{0,756},{12,24},{24,12},{36,48},{48,36},{60,72},{72,60},{84,96},{9... | collective-permute-start | bytes 147464 | tf_op jit(solution)/shard_map/ppermute | solution.py:263

commit v3 on v2

v3 whole, which is shorter than its diff:
```python
import math

import jax
import jax.numpy as jnp
from jax import lax
from jax.experimental import pallas as pl
from jax.experimental.pallas import tpu as pltpu
from jax.sharding import PartitionSpec as P

F32 = jnp.float32
BF16 = jnp.bfloat16
MIB = 1024 * 1024


def column(values):
    size = values.shape[1]
    diagonal = lax.broadcasted_iota(jnp.int32, (size, size), 0) == lax.broadcasted_iota(
        jnp.int32, (size, size), 1
    )
    spread = jnp.where(diagonal, jnp.broadcast_to(values, (size, size)).astype(F32), 0.0)
    return jnp.sum(spread, axis=1, keepdims=True)


def dot(a, b, contract):
    return lax.dot_general(a, b, (contract, ((), ())), preferred_element_type=F32)


def is_even():
    return lax.rem(lax.axis_index("dp"), 2) == 0


def prepare(
    chunk,
    inputs_hbm,
    denoiser_hbm,
    span_hbm,
    lengths_hbm,
    move_hbm,
    mode_hbm,
    sentinel_hbm,
    cotangent_hbm,
    w_query_hbm,
    w_key_hbm,
    w_value_hbm,
    shaped_ref,
    normed_ref,
    w_ref,
    marks_ref,
    own_ref,
    pay_mate_ref,
    pay_other_ref,
    inputs_v,
    span_v,
    mode_v,
    sentinel_v,
    cotangent_v,
    denoiser_s,
    lengths_s,
    move_s,
    sem,
):
    rows, length, width = inputs_v.shape
    tokens = rows * length
    chunks = width // chunk
    copies = [
        pltpu.make_async_copy(source, target, sem.at[i])
        for i, (source, target) in enumerate(
            (
                (inputs_hbm, inputs_v),
                (cotangent_hbm, cotangent_v),
                (mode_hbm, mode_v),
                (sentinel_hbm, sentinel_v),
                (span_hbm, span_v),
                (denoiser_hbm, denoiser_s),
                (lengths_hbm, lengths_s),
                (move_hbm, move_s),
                (w_query_hbm, w_ref.at[0]),
                (w_key_hbm, w_ref.at[1]),
                (w_value_hbm, w_ref.at[2]),
            )
        )
    ]
    for copy in copies:
        copy.start()
    for copy in copies[:8]:
        copy.wait()

    even = is_even()
    to_right, to_left = cotangent_v[rows + 1], cotangent_v[rows]
    pay_mate_ref[...] = jnp.where(even, to_right, to_left)
    pay_other_ref[...] = jnp.where(even, to_left, to_right)

    span = [column(span_v[r : r + 1, :]) == 1.0 for r in range(rows)]
    squares = [jnp.zeros((length, 128), F32) for _ in range(rows)]
    for c in range(chunks):
        at = pl.ds(c * chunk, chunk)
        table = mode_v[:, at].astype(F32)
        sentinel = sentinel_v[at].astype(F32).reshape(1, chunk)
        for r in range(rows):
            kind = denoiser_s[r]
            mode = jnp.where(kind == 0, table[0:1], jnp.where(kind == 1, table[1:2], table[2:3]))
            shaped = jnp.where(span[r], sentinel, inputs_v[r, :, at].astype(F32) + mode)
            shaped = shaped.astype(BF16)
            shaped_ref[r * length : (r + 1) * length, at] = shaped
            wide = shaped.astype(F32)
            wide = wide * wide
            for k in range(0, chunk, 128):
                squares[r] = squares[r] + wide[:, k : k + 128]
    mean = jnp.concatenate(squares, axis=0)
    mean = jnp.sum(mean, axis=1, keepdims=True) * (1.0 / width)
    inv_rms = lax.rsqrt(mean + 1e-06)
    for c in range(chunks):
        at = pl.ds(c * chunk, chunk)
        normed_ref[:, at] = (shaped_ref[:, at].astype(F32) * inv_rms).astype(BF16)

    t_at = lax.broadcasted_iota(jnp.int32, (length, 128), 0)
    lane = lax.broadcasted_iota(jnp.int32, (length, 128), 1)
    for r in range(rows):
        move = move_s[r]
        count = lengths_s[r]
        valid = t_at < count
        here = slice(r * length, (r + 1) * length)
        own = jnp.where(valid[:, 0:1], cotangent_v[r].astype(F32), 0.0)
        own_ref[here, :] = jnp.where(move == 0, own, 0.0).astype(BF16)
        marks = jnp.where(lane == 0, inv_rms[here], 0.0)
        marks = jnp.where((lane == 1) & valid & (move == 1), 1.0, marks)
        marks = jnp.where((lane == 2) & valid & (move == -1), 1.0, marks)
        marks = jnp.where((lane == 3) & jnp.logical_not(span[r]), 1.0, marks)
        marks = jnp.where((lane == 4) & valid & (move == 0), 1.0, marks)
        marks_ref[here, :] = jnp.where(lane == 5, jnp.maximum(count, 1).astype(F32), marks)
    for copy in copies[8:]:
        copy.wait()


def forward(
    chunk,
    rows,
    w_ref,
    normed_ref,
    marks_ref,
    wide_ref,
    soft_ref,
    context_ref,
):
    tokens, width = normed_ref.shape
    length = tokens // rows
    head = w_ref.shape[2]
    totals = []
    for i in range(3):
        total = None
        for c in range(width // chunk):
            at = pl.ds(c * chunk, chunk)
            part = dot(normed_ref[:, at], w_ref[i, at, :], ((1,), (0,)))
            total = part if total is None else total + part
        wide_ref[i] = total
        totals.append(total.astype(BF16))
    query, key, value = totals

    marks = marks_ref[...]
    factor = 1.0 / math.sqrt(head)
    q_at = lax.broadcasted_iota(jnp.int32, (tokens, tokens), 0)
    k_at = lax.broadcasted_iota(jnp.int32, (tokens, tokens), 1)
    low = jnp.where(q_at < length, 0, length)
    for r in range(2, rows):
        low = jnp.where(q_at < r * length, low, r * length)
    offset = (k_at - low).astype(F32)
    ok = (offset >= 0.0) & (offset < marks[:, 5:6])
    scores = jnp.where(ok, dot(query, key, ((1,), (1,))) * factor, -jnp.inf)
    exp_scores = jnp.exp(scores - jnp.max(scores, axis=1, keepdims=True))
    soft = exp_scores / jnp.sum(exp_scores, axis=1, keepdims=True)
    soft_ref[...] = soft
    context = dot(soft.astype(BF16), value, ((1,), (0,)))

    def only(lane):
        return jnp.where(marks[:, lane : lane + 1] == 1.0, context, 0.0)

    def one_of(picked):
        return sum(picked[r * length : (r + 1) * length] for r in range(rows)).astype(BF16)

    stays = only(4).astype(BF16)
    for r in range(rows):
        context_ref[r] = stays[r * length : (r + 1) * length]
    context_ref[rows] = one_of(only(1))
    context_ref[rows + 1] = one_of(only(2))


def emit(chunk, gradients, w_ref, shaped_ref, inv_rms, inner, keep, out_ref):
    pieces, rows, per_row, width = out_ref.shape
    length = shaped_ref.shape[0] // rows
    scale = jnp.where(keep, inv_rms, 0.0)
    back = inv_rms * inner
    for c in range(width // chunk):
        at = pl.ds(c * chunk, chunk)
        total = None
        for i in range(3):
            part = dot(gradients[i], w_ref[i, at, :], ((1,), (1,)))
            total = part if total is None else total + part
        part = ((total - shaped_ref[:, at].astype(F32) * back) * scale).astype(BF16)
        for d in range(pieces):
            for r in range(rows):
                low = r * length + d * per_row
                out_ref[d, r, :, at] = part[low : low + per_row]


def backward(
    chunk,
    w_ref,
    shaped_ref,
    marks_ref,
    wide_ref,
    soft_ref,
    own_ref,
    context_ref,
    got_mate_ref,
    got_other_ref,
    out_ref,
    pay_mate_ref,
    pay_other_ref,
):
    rows = out_ref.shape[1]
    width = shaped_ref.shape[1]
    head = w_ref.shape[2]

    even = is_even()
    right, left = context_ref[rows], context_ref[rows + 1]
    pay_mate_ref[...] = jnp.where(even, right, left)
    pay_other_ref[...] = jnp.where(even, left, right)
    from_right = jnp.where(even, got_mate_ref[...], got_other_ref[...]).astype(F32)
    from_left = jnp.where(even, got_other_ref[...], got_mate_ref[...]).astype(F32)
    marks = marks_ref[...]
    inv_rms = marks[:, 0:1]
    grad_out = jnp.where(
        marks[:, 1:2] == 1.0,
        jnp.concatenate([from_right] * rows, axis=0),
        jnp.where(
            marks[:, 2:3] == 1.0,
            jnp.concatenate([from_left] * rows, axis=0),
            own_ref[...].astype(F32),
        ),
    ).astype(BF16)

    factor = 1.0 / math.sqrt(head)
    soft = soft_ref[...]
    query, key, value = (wide_ref[i].astype(BF16) for i in range(3))
    grad_value = dot(soft.astype(BF16), grad_out, ((0,), (0,))).astype(BF16)
    grad_soft = dot(grad_out, value, ((1,), (1,)))
    row_inner = jnp.sum(soft * grad_soft, axis=1, keepdims=True)
    grad_scores = (soft * (grad_soft - row_inner) * factor).astype(BF16)
    grad_query = dot(grad_scores, key, ((1,), (0,))).astype(BF16)
    grad_key = dot(grad_scores, query, ((0,), (0,))).astype(BF16)
    gradients = (grad_query, grad_key, grad_value)
    inner = sum(gradients[i].astype(F32) * wide_ref[i] for i in range(3))
    inner = jnp.sum(inner, axis=1, keepdims=True) * (1.0 / width)
    emit(chunk, gradients, w_ref, shaped_ref, inv_rms, inner, marks[:, 3:4] == 1.0, out_ref)


def assemble(context_ref, got_mate_ref, got_other_ref, out_ref):
    rows = context_ref.shape[0] // 2
    even = is_even()
    got_mate = got_mate_ref[...]
    got_other = got_other_ref[...]
    for r in range(rows):
        out_ref[r] = context_ref[r]
    out_ref[rows] = jnp.where(even, got_other, got_mate)
    out_ref[rows + 1] = jnp.where(even, got_mate, got_other)


def add_heads(heads_ref, out_ref):
    total = heads_ref[0].astype(F32)
    for h in range(1, heads_ref.shape[0]):
        total = total + heads_ref[h].astype(F32)
    out_ref[...] = total.astype(BF16)


def exchange(array, pairs):
    return lax.ppermute(array, "dp", pairs)


def shards(
    inputs,
    denoiser,
    span_mask,
    lengths,
    move_plan,
    mode_table,
    sentinel,
    w_query,
    w_key,
    w_value,
    cotangent,
):
    rows, length, width = inputs.shape
    head = w_query.shape[1]
    tokens = rows * length
    groups = lax.axis_size("dp")
    members = lax.axis_size("mp")
    seg = length // members
    chunk = 512
    vmem = pl.BlockSpec(memory_space=pltpu.VMEM)
    hbm = pl.BlockSpec(memory_space=pltpu.HBM)
    params = pltpu.CompilerParams(vmem_limit_bytes=24 * MIB)
    mates = [(g, g ^ 1) for g in range(groups)]
    others = [(g, (g + 1) % groups if g % 2 else (g - 1) % groups) for g in range(groups)]

    def shape(dims, dtype):
        return jax.ShapeDtypeStruct(dims, dtype)

    slot = shape((length, head), BF16)
    shaped, normed, w_all, marks, own, pay_mate, pay_other = pl.pallas_call(
        lambda *refs: prepare(chunk, *refs),
        out_shape=(
            shape((tokens, width), BF16),
            shape((tokens, width), BF16),
            shape((3, width, head), BF16),
            shape((tokens, 128), F32),
            shape((tokens, head), BF16),
            slot,
            slot,
        ),
        in_specs=[hbm] * 11,
        out_specs=[vmem] * 7,
        scratch_shapes=[
            pltpu.VMEM((rows, length, width), BF16),
            pltpu.VMEM(span_mask.shape, jnp.int32),
            pltpu.VMEM(mode_table.shape, BF16),
            pltpu.VMEM((width,), BF16),
            pltpu.VMEM(cotangent.shape, BF16),
            pltpu.SMEM((rows,), jnp.int32),
            pltpu.SMEM((rows,), jnp.int32),
            pltpu.SMEM((rows,), jnp.int32),
            pltpu.SemaphoreType.DMA((11,)),
        ],
        compiler_params=params,
        name="prepare",
    )(
        *(
            pltpu.with_memory_space_constraint(array, pltpu.HBM)
            for array in (
                inputs,
                denoiser,
                span_mask,
                lengths,
                move_plan,
                mode_table,
                sentinel,
                cotangent,
                w_query,
                w_key,
                w_value,
            )
        )
    )
    cotangent_other = exchange(pay_other, others)
    cotangent_mate = exchange(pay_mate, mates)

    wide, soft, context = pl.pallas_call(
        lambda *refs: forward(chunk, rows, *refs),
        out_shape=(
            shape((3, tokens, head), F32),
            shape((tokens, tokens), F32),
            shape((2 * rows, length, head), BF16),
        ),
        in_specs=[vmem] * 3,
        out_specs=[vmem] * 3,
        compiler_params=params,
        name="forward",
    )(w_all, normed, marks)

    head_part, pay_mate, pay_other = pl.pallas_call(
        lambda *refs: backward(chunk, *refs),
        out_shape=(shape((members, rows, seg, width), BF16), slot, slot),
        in_specs=[vmem] * 9,
        out_specs=[vmem] * 3,
        compiler_params=params,
        name="backward",
    )(
        w_all,
        shaped,
        marks,
        wide,
        soft,
        own,
        context,
        cotangent_mate,
        cotangent_other,
    )
    heads = lax.all_to_all(head_part, "mp", 0, 0)
    got_other = exchange(pay_other, others)
    got_mate = exchange(pay_mate, mates)
    context = pl.pallas_call(
        assemble,
        out_shape=shape(context.shape, BF16),
        in_specs=[vmem] * 3,
        out_specs=vmem,
        name="assemble",
    )(context, got_mate, got_other)
    input_grad = pl.pallas_call(
        add_heads,
        out_shape=shape((rows, seg, width), BF16),
        in_specs=[vmem],
        out_specs=vmem,
        compiler_params=params,
        name="add_heads",
    )(heads)
    return (context, input_grad)


def solution(mesh):
    return jax.shard_map(
        shards,
        mesh=mesh,
        in_specs=(
            P("dp", None, None),
            P("dp"),
            P("dp", None),
            P("dp"),
            P("dp"),
            P(),
            P(),
            P(None, "mp"),
            P(None, "mp"),
            P(None, "mp"),
            P("dp", None, "mp"),
        ),
        out_specs=(P("dp", None, "mp"), P("dp", "mp", None)),
        check_vma=False,
    )
```

time: 68.4 us -> 64.4 us (0.942)
  the two profiles are of different devices: /device:TPU:63 before, /device:TPU:25 now
where the time goes in v3:
time: 64.4 us; the launch traced here: 64 us
  starting transfers between devices  28.3 us (44%)
  waiting for transfers between devices  23.9 us (37%)
  Pallas kernels  10.5 us (16%)
  between operations  0.72 us (1%)
    all_to_all x1, waiting for transfers between devices, shards(): heads = lax.all_to_all(head_part, 'mp', 0, 0)  21.4 us
    all_to_all x1, starting transfers between devices, shards(): heads = lax.all_to_all(head_part, 'mp', 0, 0)  14.9 us
    ppermute x4, starting transfers between devices, exchange(): return lax.ppermute(array, 'dp', pairs)  13.4 us
    pallas_call x1, Pallas kernels, shards(): pl.pallas_call(lambda *refs: backward(chunk, *refs), out_shape=(shape((me...  3.35 us
    pallas_call x1, Pallas kernels, shards(): pl.pallas_call(lambda *refs: prepare(chunk, *refs), out_shape=(shape((tok...  3.29 us
    ppermute x4, waiting for transfers between devices, exchange(): return lax.ppermute(array, 'dp', pairs)  2.51 us
    pallas_call x1, Pallas kernels, shards(): pl.pallas_call(assemble, out_shape=shape(context.shape, BF16), in_specs=[...  1.56 us
    pallas_call x1, Pallas kernels, shards(): pl.pallas_call(lambda *refs: forward(chunk, rows, *refs), out_shape=(shap...  1.53 us
  transfers between devices with their start and end apart: 5, of which 3 were waited for; matrix products, arithmetic and copies ran while one was open for 0% of the time, Pallas kernels for 5%

profile of v3, /device:TPU:25, one launch (start us, length us, event | category | flops | bytes accessed | tf_op | source)
XLA Modules:
  0.0 64.0 jit_solution(11167629750065469230)
XLA Ops:
  0.6 3.3 %prepare.1 = (bf16[96,4096]{1,0:T(8,128)(2,1)S(1)}, bf16[96,4096]{1,0:T(8,128)(2,1)S(1)}, bf16[3,4096,256]{2,1,0:T(8,128)(2,1)S(1)}, f32[96,128]{1,0:T(8,128)S(1...) custom-call(bf16[2,48,4096]{2,1,0:T(8,128)(2,1)} %refs_0_.1, s32[2]{0:T(128)} %refs_1_.1, ...), custom_call_target="tpu_custom_call" | custom-call | tf_op jit(solution)/shard_map/prepare/pallas_call | solution.py:309
  3.9 2.6 %collective-permute-start = (bf16[48,256]{1,0:T(8,128)(2,1)S(1)}, bf16[48,256]{1,0:T(8,128)(2,1)S(1)}, u32[]{:S(2)}, u32[]{:S(2)}) collective-permute-start(bf16[48,256]{1,0:T(8,128)(2,1)S(1)} %get-tuple-element.23), channel_id=1, source_target_pairs={{0,12},{12,0},{24,36},{36,24},{48,60},{60,48},{72,84},{84,72},{96,... | collective-permute-start | bytes 73736 | tf_op jit(solution)/shard_map/ppermute | solution.py:276
  6.5 4.3 %collective-permute-start.1 = (bf16[48,256]{1,0:T(8,128)(2,1)S(1)}, bf16[48,256]{1,0:T(8,128)(2,1)S(1)}, u32[]{:S(2)}, u32[]{:S(2)}) collective-permute-start(bf16[48,256]{1,0:T(8,128)(2,1)S(1)} %get-tuple-element.24), channel_id=1, source_target_pairs={{0,756},{12,24},{24,12},{36,48},{48,36},{60,72},{72,60},{84,96},{9... | collective-permute-start | bytes 73736 | tf_op jit(solution)/shard_map/ppermute | solution.py:276
  10.8 1.5 %forward.1 = (f32[3,96,256]{2,1,0:T(8,128)S(1)}, f32[96,96]{1,0:T(8,128)S(1)}, bf16[4,48,256]{2,1,0:T(8,128)(2,1)S(1)}) custom-call(bf16[3,4096,256]{2,1,0:T(8,128)(2,1)S(1)} %get-tuple-element.15.refs_0_, bf16[96,4096]{1,0:T(8,128)(2,1)S(1)} %get-tuple-element.16.refs_1_, f32[96,128]{1,0:T(8,128)S(1)} %get-tuple-element.17.refs_2_), custom_call_target="tpu_custom_call" | custom-call | tf_op jit(solution)/shard_map/forward/pallas_call | solution.py:356
  12.4 0.0 copy-start
  12.4 0.0 collective-permute-done.refs_7_
  12.4 0.5 collective-permute-done.1.refs_8_
  12.9 3.3 %backward.1 = (bf16[12,2,4,4096]{3,2,1,0:T(4,128)(2,1)}, bf16[48,256]{1,0:T(8,128)(2,1)S(1)}, bf16[48,256]{1,0:T(8,128)(2,1)S(1)}) custom-call(bf16[3,4096,256]{2,1,0:T(8,128)(2,1)S(1)} %get-tuple-element.15.refs_0_, bf16[96,4096]{1,0:T(8,128)(2,1)S(1)} %get-tuple-element.19.refs_1_, f32[96,128]{1,0:T(8,128)S(1)} %get-tuple-element.17.refs_2_, ...), custom_call_target="tpu_custom_call" | custom-call | tf_op jit(solution)/shard_map/backward/pallas_call | solution.py:369
  16.2 0.0 copy-done
  16.2 14.9 %all-to-all-start = ((bf16[12,2,4,4096]{3,2,1,0:T(4,128)(2,1)}), bf16[12,2,4,4096]{3,2,1,0:T(4,128)(2,1)S(1)}, u32[]{:S(2)}, u32[]{:S(2)}) async-start(bf16[12,2,4,4096]{3,2,1,0:T(4,128)(2,1)} %get-tuple-element.27), calls=%async_computation | async-start | bytes 1572864 | tf_op jit(solution)/shard_map/all_to_all | solution.py:387
  31.1 1.9 %collective-permute-start.2 = (bf16[48,256]{1,0:T(8,128)(2,1)S(1)}, bf16[48,256]{1,0:T(8,128)(2,1)S(1)}, u32[]{:S(2)}, u32[]{:S(2)}) collective-permute-start(bf16[48,256]{1,0:T(8,128)(2,1)S(1)} %get-tuple-element.25), channel_id=1, source_target_pairs={{0,12},{12,0},{24,36},{36,24},{48,60},{60,48},{72,84},{84,72},{96,... | collective-permute-start | bytes 73736 | tf_op jit(solution)/shard_map/ppermute | solution.py:276
  33.0 4.6 %collective-permute-start.3 = (bf16[48,256]{1,0:T(8,128)(2,1)S(1)}, bf16[48,256]{1,0:T(8,128)(2,1)S(1)}, u32[]{:S(2)}, u32[]{:S(2)}) collective-permute-start(bf16[48,256]{1,0:T(8,128)(2,1)S(1)} %get-tuple-element.26), channel_id=1, source_target_pairs={{0,756},{12,24},{24,12},{36,48},{48,36},{60,72},{72,60},{84,96},{9... | collective-permute-start | bytes 73736 | tf_op jit(solution)/shard_map/ppermute | solution.py:276
  37.6 0.0 collective-permute-done.2.got_mate_ref
  37.7 0.0 copy-start.1
  37.7 2.0 %collective-permute-done.3.got_other_ref = bf16[48,256]{1,0:T(8,128)(2,1)S(1)} collective-permute-done((bf16[48,256]{1,0:T(8,128)(2,1)S(1)}, bf16[48,256]{1,0:T(8,128)(2,1)S(1)}, u32[]{:S(2)}, u32[]{:S(2)}) %collective-permute-start.3) | collective-permute-done | bytes 24608 | tf_op jit(solution)/shard_map/ppermute | solution.py:276
  39.7 0.0 copy-done.1
  39.7 0.0 copy-start.2
  39.7 0.6 copy-done.2
  40.3 1.6 %assemble.1 = bf16[4,48,256]{2,1,0:T(8,128)(2,1)} custom-call(bf16[4,48,256]{2,1,0:T(8,128)(2,1)} %copy-done, bf16[48,256]{1,0:T(8,128)(2,1)} %copy-done.1, bf16[48,256]{1,0:T(8,128)(2,1)} %copy-done.2), custom_call_target="tpu_custom_call" | custom-call | tf_op jit(solution)/shard_map/assemble/pallas_call | solution.py:390
  41.9 21.4 %all-to-all-done.heads_ref = bf16[12,2,4,4096]{3,2,1,0:T(4,128)(2,1)S(1)} async-done(((bf16[12,2,4,4096]{3,2,1,0:T(4,128)(2,1)}), bf16[12,2,4,4096]{3,2,1,0:T(4,128)(2,1)S(1)}, u32[]{:S(2)}, u32[]{:S(2)}) %all-to-all-start) | async-done | bytes 786464 | tf_op jit(solution)/shard_map/all_to_all | solution.py:387
  63.3 0.7 %add_heads.1 = bf16[2,4,4096]{2,1,0:T(4,128)(2,1)} custom-call(bf16[12,2,4,4096]{3,2,1,0:T(4,128)(2,1)S(1)} %all-to-all-done.heads_ref), custom_call_target="tpu_custom_call" | custom-call | tf_op jit(solution)/shard_map/add_heads/pallas_call | solution.py:397
Async XLA Ops:
  3.9 8.5 %collective-permute-start = (bf16[48,256]{1,0:T(8,128)(2,1)S(1)}, bf16[48,256]{1,0:T(8,128)(2,1)S(1)}, u32[]{:S(2)}, u32[]{:S(2)}) collective-permute-start(bf16[48,256]{1,0:T(8,128)(2,1)S(1)} %get-tuple-element.23), channel_id=1, source_target_pairs={{0,12},{12,0},{24,36},{36,24},{48,60},{60,48},{72,84},{84,72},{96,... | collective-permute-start | bytes 73736 | tf_op jit(solution)/shard_map/ppermute | solution.py:276
  6.5 6.4 %collective-permute-start.1 = (bf16[48,256]{1,0:T(8,128)(2,1)S(1)}, bf16[48,256]{1,0:T(8,128)(2,1)S(1)}, u32[]{:S(2)}, u32[]{:S(2)}) collective-permute-start(bf16[48,256]{1,0:T(8,128)(2,1)S(1)} %get-tuple-element.24), channel_id=1, source_target_pairs={{0,756},{12,24},{24,12},{36,48},{48,36},{60,72},{72,60},{84,96},{9... | collective-permute-start | bytes 73736 | tf_op jit(solution)/shard_map/ppermute | solution.py:276
  12.4 3.9 %copy-start = (bf16[4,48,256]{2,1,0:T(8,128)(2,1)}, bf16[4,48,256]{2,1,0:T(8,128)(2,1)S(1)}, u32[]{:S(2)}) copy-start(bf16[4,48,256]{2,1,0:T(8,128)(2,1)S(1)} %get-tuple-element.18.refs_6_.context_ref) | copy-start | bytes 294916
  16.2 47.1 %all-to-all-start = ((bf16[12,2,4,4096]{3,2,1,0:T(4,128)(2,1)}), bf16[12,2,4,4096]{3,2,1,0:T(4,128)(2,1)S(1)}, u32[]{:S(2)}, u32[]{:S(2)}) async-start(bf16[12,2,4,4096]{3,2,1,0:T(4,128)(2,1)} %get-tuple-element.27), calls=%async_computation | async-start | bytes 1572864 | tf_op jit(solution)/shard_map/all_to_all | solution.py:387
  31.1 6.5 %collective-permute-start.2 = (bf16[48,256]{1,0:T(8,128)(2,1)S(1)}, bf16[48,256]{1,0:T(8,128)(2,1)S(1)}, u32[]{:S(2)}, u32[]{:S(2)}) collective-permute-start(bf16[48,256]{1,0:T(8,128)(2,1)S(1)} %get-tuple-element.25), channel_id=1, source_target_pairs={{0,12},{12,0},{24,36},{36,24},{48,60},{60,48},{72,84},{84,72},{96,... | collective-permute-start | bytes 73736 | tf_op jit(solution)/shard_map/ppermute | solution.py:276
  33.0 6.7 %collective-permute-start.3 = (bf16[48,256]{1,0:T(8,128)(2,1)S(1)}, bf16[48,256]{1,0:T(8,128)(2,1)S(1)}, u32[]{:S(2)}, u32[]{:S(2)}) collective-permute-start(bf16[48,256]{1,0:T(8,128)(2,1)S(1)} %get-tuple-element.26), channel_id=1, source_target_pairs={{0,756},{12,24},{24,12},{36,48},{48,36},{60,72},{72,60},{84,96},{9... | collective-permute-start | bytes 73736 | tf_op jit(solution)/shard_map/ppermute | solution.py:276
  37.7 2.0 %copy-start.1 = (bf16[48,256]{1,0:T(8,128)(2,1)}, bf16[48,256]{1,0:T(8,128)(2,1)S(1)}, u32[]{:S(2)}) copy-start(bf16[48,256]{1,0:T(8,128)(2,1)S(1)} %collective-permute-done.2.got_mate_ref) | copy-start | bytes 73732
  39.7 0.6 copy-start.2

commit v4 on v3

--- a/solution.py
+++ b/solution.py
@@ -10,6 +10,7 @@
 F32 = jnp.float32
 BF16 = jnp.bfloat16
 MIB = 1024 * 1024
+WINDOW = 3
 
 
 def column(values):
@@ -184,11 +185,29 @@
     context_ref[rows + 1] = one_of(only(2))
 
 
-def emit(chunk, gradients, w_ref, shaped_ref, inv_rms, inner, keep, out_ref):
-    pieces, rows, per_row, width = out_ref.shape
-    length = shaped_ref.shape[0] // rows
+def order_rows(tokens, rows, members):
+    per_row = tokens // rows // members
+    piece = rows * per_row
+    row_at = lax.broadcasted_iota(jnp.int32, (tokens, tokens), 0)
+    from_at = lax.broadcasted_iota(jnp.int32, (tokens, tokens), 1)
+    mine = lax.rem(lax.axis_index("mp"), WINDOW)
+    want = jnp.full((tokens, tokens), -1, jnp.int32)
+    for i in range(tokens // per_row):
+        block, left = divmod(i, tokens // WINDOW // per_row)
+        j, r = divmod(left, rows)
+        member = WINDOW * j + lax.rem(mine + block, WINDOW)
+        first = r * (tokens // rows) + member * per_row
+        here = (row_at >= i * per_row) & (row_at < (i + 1) * per_row)
+        want = jnp.where(here, first + row_at - i * per_row, want)
+    return jnp.where(from_at == want, 1.0, 0.0).astype(BF16)
+
+
+def emit(chunk, rows, gradients, w_ref, shaped_ref, inv_rms, inner, keep, out_refs):
+    tokens, width = shaped_ref.shape
+    pieces, piece, _ = out_refs[0].shape
     scale = jnp.where(keep, inv_rms, 0.0)
     back = inv_rms * inner
+    order = order_rows(tokens, rows, pieces * WINDOW)
     for c in range(width // chunk):
         at = pl.ds(c * chunk, chunk)
         total = None
@@ -196,10 +215,11 @@
             part = dot(gradients[i], w_ref[i, at, :], ((1,), (1,)))
             total = part if total is None else total + part
         part = ((total - shaped_ref[:, at].astype(F32) * back) * scale).astype(BF16)
-        for d in range(pieces):
-            for r in range(rows):
-                low = r * length + d * per_row
-                out_ref[d, r, :, at] = part[low : low + per_row]
+        part = dot(order, part, ((1,), (0,))).astype(BF16)
+        for s in range(WINDOW):
+            for j in range(pieces):
+                low = (s * pieces + j) * piece
+                out_refs[s][j, :, at] = part[low : low + piece]
 
 
 def backward(
@@ -210,21 +230,15 @@
     wide_ref,
     soft_ref,
     own_ref,
-    context_ref,
     got_mate_ref,
     got_other_ref,
-    out_ref,
-    pay_mate_ref,
-    pay_other_ref,
+    *out_refs,
 ):
-    rows = out_ref.shape[1]
-    width = shaped_ref.shape[1]
+    tokens, width = shaped_ref.shape
+    rows = tokens // got_mate_ref.shape[0]
     head = w_ref.shape[2]
 
     even = is_even()
-    right, left = context_ref[rows], context_ref[rows + 1]
-    pay_mate_ref[...] = jnp.where(even, right, left)
-    pay_other_ref[...] = jnp.where(even, left, right)
     from_right = jnp.where(even, got_mate_ref[...], got_other_ref[...]).astype(F32)
     from_left = jnp.where(even, got_other_ref[...], got_mate_ref[...]).astype(F32)
     marks = marks_ref[...]
@@ -251,25 +265,40 @@
     gradients = (grad_query, grad_key, grad_value)
     inner = sum(gradients[i].astype(F32) * wide_ref[i] for i in range(3))
     inner = jnp.sum(inner, axis=1, keepdims=True) * (1.0 / width)
-    emit(chunk, gradients, w_ref, shaped_ref, inv_rms, inner, marks[:, 3:4] == 1.0, out_ref)
-
-
-def assemble(context_ref, got_mate_ref, got_other_ref, out_ref):
+    emit(chunk, rows, gradients, w_ref, shaped_ref, inv_rms, inner, marks[:, 3:4] == 1.0, out_refs)
+
+
+def combine(
+    keep_ref, got_left_ref, got_right_ref, context_ref, got_mate_ref, out_ref, pay_other_ref
+):
+    del got_mate_ref
+    total = keep_ref[...].astype(F32) + got_left_ref[...].astype(F32)
+    out_ref[...] = (total + got_right_ref[...].astype(F32)).astype(BF16)
+    rows = context_ref.shape[0] // 2
+    pay_other_ref[...] = jnp.where(is_even(), context_ref[rows + 1], context_ref[rows])
+
+
+def address(keep_ref, context_ref, pay_mate_ref):
+    del keep_ref
+    rows = context_ref.shape[0] // 2
+    pay_mate_ref[...] = jnp.where(is_even(), context_ref[rows], context_ref[rows + 1])
+
+
+def finish(heads_ref, context_ref, got_mate_ref, got_other_ref, context_out_ref, out_ref):
     rows = context_ref.shape[0] // 2
     even = is_even()
     got_mate = got_mate_ref[...]
     got_other = got_other_ref[...]
     for r in range(rows):
-        out_ref[r] = context_ref[r]
-    out_ref[rows] = jnp.where(even, got_other, got_mate)
-    out_ref[rows + 1] = jnp.where(even, got_mate, got_other)
-
-
-def add_heads(heads_ref, out_ref):
+        context_out_ref[r] = context_ref[r]
+    context_out_ref[rows] = jnp.where(even, got_other, got_mate)
+    context_out_ref[rows + 1] = jnp.where(even, got_mate, got_other)
     total = heads_ref[0].astype(F32)
     for h in range(1, heads_ref.shape[0]):
         total = total + heads_ref[h].astype(F32)
-    out_ref[...] = total.astype(BF16)
+    per_row = out_ref.shape[1]
+    for r in range(out_ref.shape[0]):
+        out_ref[r] = total[r * per_row : (r + 1) * per_row].astype(BF16)
 
 
 def exchange(array, pairs):
@@ -366,42 +395,45 @@
         name="forward",
     )(w_all, normed, marks)
 
-    head_part, pay_mate, pay_other = pl.pallas_call(
-        lambda *refs: backward(chunk, *refs),
-        out_shape=(shape((members, rows, seg, width), BF16), slot, slot),
-        in_specs=[vmem] * 9,
+    part = shape((members // WINDOW, rows * seg, width), BF16)
+    keep, to_right, to_left = pl.pallas_call(
+        lambda *refs: backward(width, *refs),
+        out_shape=(part, part, part),
+        in_specs=[vmem] * 8,
         out_specs=[vmem] * 3,
         compiler_params=params,
         name="backward",
-    )(
-        w_all,
-        shaped,
-        marks,
-        wide,
-        soft,
-        own,
-        context,
-        cotangent_mate,
-        cotangent_other,
-    )
-    heads = lax.all_to_all(head_part, "mp", 0, 0)
+    )(w_all, shaped, marks, wide, soft, own, cotangent_mate, cotangent_other)
+    from_left = lax.ppermute(to_right, "mp", [(m, (m + 1) % members) for m in range(members)])
+    from_right = lax.ppermute(to_left, "mp", [(m, (m - 1) % members) for m in range(members)])
+    pay_mate = pl.pallas_call(
+        address,
+        out_shape=slot,
+        in_specs=[vmem] * 2,
+        out_specs=vmem,
+        compiler_params=params,
+        name="address",
+    )(keep, context)
+    got_mate = exchange(pay_mate, mates)
+    windows, pay_other = pl.pallas_call(
+        combine,
+        out_shape=(part, slot),
+        in_specs=[vmem] * 5,
+        out_specs=[vmem] * 2,
+        compiler_params=params,
+        name="combine",
+    )(keep, from_left, from_right, context, got_mate)
     got_other = exchange(pay_other, others)
-    got_mate = exchange(pay_mate, mates)
-    context = pl.pallas_call(
-        assemble,
-        out_shape=shape(context.shape, BF16),
-        in_specs=[vmem] * 3,
-        out_specs=vmem,
-        name="assemble",
-    )(context, got_mate, got_other)
-    input_grad = pl.pallas_call(
-        add_heads,
-        out_shape=shape((rows, seg, width), BF16),
-        in_specs=[vmem],
-        out_specs=vmem,
-        compiler_params=params,
-        name="add_heads",
-    )(heads)
+    spread = [list(range(c, members, WINDOW)) for c in range(WINDOW)]
+    heads = lax.all_to_all(windows, "mp", 0, 0, axis_index_groups=spread)
+    context, input_grad = pl.pallas_call(
+        finish,
+        out_shape=(shape(context.shape, BF16), shape((rows, seg, width), BF16)),
+        in_specs=[vmem] * 4,
+        out_specs=[vmem] * 2,
+        compiler_params=params,
+        name="finish",
+    )(heads, context, got_mate, got_other)
     return (context, input_grad)
 
 

time: 64.4 us -> 60.8 us (0.944)
  the two profiles are of different devices: /device:TPU:25 before, /device:TPU:63 now
where the time goes in v4:
time: 60.8 us; the launch traced here: 60.4 us
  starting transfers between devices  36.8 us (61%)
  waiting for transfers between devices  13.8 us (23%)
  Pallas kernels  9.04 us (15%)
  between operations  0.73 us (1%)
    ppermute x4, starting transfers between devices, exchange(): return lax.ppermute(array, 'dp', pairs)  18.2 us
    ppermute x1, starting transfers between devices, shards(): lax.ppermute(to_left, 'mp', [(m, (m - 1) % members) for m in range(member...  11 us
    all_to_all x1, waiting for transfers between devices, shards(): heads = lax.all_to_all(windows, 'mp', 0, 0, axis_index_groups=spread)  7.18 us
    ppermute x4, waiting for transfers between devices, exchange(): return lax.ppermute(array, 'dp', pairs)  6.46 us
    all_to_all x1, starting transfers between devices, shards(): heads = lax.all_to_all(windows, 'mp', 0, 0, axis_index_groups=spread)  5.76 us
    pallas_call x1, Pallas kernels, shards(): pl.pallas_call(lambda *refs: prepare(chunk, *refs), out_shape=(shape((tok...  3.29 us
    pallas_call x1, Pallas kernels, shards(): pl.pallas_call(lambda *refs: backward(width, *refs), out_shape=(part, par...  2.71 us
    ppermute x1, starting transfers between devices, shards(): lax.ppermute(to_right, 'mp', [(m, (m + 1) % members) for m in range(membe...  1.92 us
  transfers between devices with their start and end apart: 7, of which 4 were waited for; matrix products, arithmetic and copies ran while one was open for 0% of the time, Pallas kernels for 3%

profile of v4, /device:TPU:63, one launch (start us, length us, event | category | flops | bytes accessed | tf_op | source)
XLA Modules:
  0.0 60.4 jit_solution(1096465789306350018)
XLA Ops:
  0.6 3.3 %prepare.1 = (bf16[96,4096]{1,0:T(8,128)(2,1)S(1)}, bf16[96,4096]{1,0:T(8,128)(2,1)S(1)}, bf16[3,4096,256]{2,1,0:T(8,128)(2,1)S(1)}, f32[96,128]{1,0:T(8,128)S(1...) custom-call(bf16[2,48,4096]{2,1,0:T(8,128)(2,1)} %refs_0_.1, s32[2]{0:T(128)} %refs_1_.1, ...), custom_call_target="tpu_custom_call" | custom-call | tf_op jit(solution)/shard_map/prepare/pallas_call | solution.py:338
  3.9 2.6 %collective-permute-start = (bf16[48,256]{1,0:T(8,128)(2,1)S(1)}, bf16[48,256]{1,0:T(8,128)(2,1)S(1)}, u32[]{:S(2)}, u32[]{:S(2)}) collective-permute-start(bf16[48,256]{1,0:T(8,128)(2,1)S(1)} %get-tuple-element.24), channel_id=1, source_target_pairs={{0,12},{12,0},{24,36},{36,24},{48,60},{60,48},{72,84},{84,72},{96,... | collective-permute-start | bytes 73736 | tf_op jit(solution)/shard_map/ppermute | solution.py:305
  6.5 10.2 %collective-permute-start.1 = (bf16[48,256]{1,0:T(8,128)(2,1)S(1)}, bf16[48,256]{1,0:T(8,128)(2,1)S(1)}, u32[]{:S(2)}, u32[]{:S(2)}) collective-permute-start(bf16[48,256]{1,0:T(8,128)(2,1)S(1)} %get-tuple-element.25), channel_id=1, source_target_pairs={{0,756},{12,24},{24,12},{36,48},{48,36},{60,72},{72,60},{84,96},{9... | collective-permute-start | bytes 73736 | tf_op jit(solution)/shard_map/ppermute | solution.py:305
  16.7 1.5 %forward.1 = (f32[3,96,256]{2,1,0:T(8,128)S(1)}, f32[96,96]{1,0:T(8,128)S(1)}, bf16[4,48,256]{2,1,0:T(8,128)(2,1)S(1)}) custom-call(bf16[3,4096,256]{2,1,0:T(8,128)(2,1)S(1)} %get-tuple-element.17.refs_0_, bf16[96,4096]{1,0:T(8,128)(2,1)S(1)} %get-tuple-element.20.refs_1_, f32[96,128]{1,0:T(8,128)S(1)} %get-tuple-element.19.refs_2_), custom_call_target="tpu_custom_call" | custom-call | tf_op jit(solution)/shard_map/forward/pallas_call | solution.py:385
  18.3 0.0 collective-permute-done.refs_6_
  18.3 0.0 collective-permute-done.1.refs_7_
  18.3 2.7 %backward.1 = (bf16[4,8,4096]{2,1,0:T(8,128)(2,1)S(1)}, bf16[4,8,4096]{2,1,0:T(8,128)(2,1)S(1)}, bf16[4,8,4096]{2,1,0:T(8,128)(2,1)S(1)}) custom-call(bf16[3,4096,256]{2,1,0:T(8,128)(2,1)S(1)} %get-tuple-element.17.refs_0_, bf16[96,4096]{1,0:T(8,128)(2,1)S(1)} %get-tuple-element.18.refs_1_, f32[96,128]{1,0:T(8,128)S(1)} %get-tuple-element.19.refs_2_, ...), custom_call_target="tpu_custom_call" | custom-call | tf_op jit(solution)/shard_map/backward/pallas_call | solution.py:399
  21.0 1.9 %collective-permute-start.2 = (bf16[4,8,4096]{2,1,0:T(8,128)(2,1)S(1)}, bf16[4,8,4096]{2,1,0:T(8,128)(2,1)S(1)}, u32[]{:S(2)}, u32[]{:S(2)}) collective-permute-start(bf16[4,8,4096]{2,1,0:T(8,128)(2,1)S(1)} %get-tuple-element.27), channel_id=1, source_target_pairs={{0,1},{1,2},{2,3},{3,4},{4,5},{5,6},{6,7},{7,8},{8,9},{9,10},{10,1... | collective-permute-start | bytes 786440 | tf_op jit(solution)/shard_map/ppermute | solution.py:407
  23.0 11.0 %collective-permute-start.3 = (bf16[4,8,4096]{2,1,0:T(8,128)(2,1)S(1)}, bf16[4,8,4096]{2,1,0:T(8,128)(2,1)S(1)}, u32[]{:S(2)}, u32[]{:S(2)}) collective-permute-start(bf16[4,8,4096]{2,1,0:T(8,128)(2,1)S(1)} %get-tuple-element.28), channel_id=1, source_target_pairs={{0,11},{1,0},{2,1},{3,2},{4,3},{5,4},{6,5},{7,6},{8,7},{9,8},{10,9... | collective-permute-start | bytes 786440 | tf_op jit(solution)/shard_map/ppermute | solution.py:408
  34.0 1.9 %collective-permute-start.4 = (bf16[48,256]{1,0:T(8,128)(2,1)S(1)}, bf16[48,256]{1,0:T(8,128)(2,1)S(1)}, u32[]{:S(2)}, u32[]{:S(2)}) collective-permute-start(bf16[48,256]{1,0:T(8,128)(2,1)S(1)} %address.1), channel_id=1, source_target_pairs={{0,12},{12,0},{24,36},{36,24},{48,60},{60,48},{72,84},{84,72},{96,... | collective-permute-start | bytes 73736 | tf_op jit(solution)/shard_map/ppermute | solution.py:305
  35.9 1.2 %collective-permute-done.4.got_mate_ref = bf16[48,256]{1,0:T(8,128)(2,1)S(1)} collective-permute-done((bf16[48,256]{1,0:T(8,128)(2,1)S(1)}, bf16[48,256]{1,0:T(8,128)(2,1)S(1)}, u32[]{:S(2)}, u32[]{:S(2)}) %collective-permute-start.4) | collective-permute-done | bytes 24608 | tf_op jit(solution)/shard_map/ppermute | solution.py:305
  37.1 0.0 collective-permute-done.2.got_left_ref
  37.1 0.2 collective-permute-done.3.got_right_ref
  37.2 0.8 %combine.1 = (bf16[4,8,4096]{2,1,0:T(8,128)(2,1)}, bf16[48,256]{1,0:T(8,128)(2,1)S(1)}) custom-call(bf16[4,8,4096]{2,1,0:T(8,128)(2,1)S(1)} %get-tuple-element.26.keep_ref, bf16[4,8,4096]{2,1,0:T(8,128)(2,1)S(1)} %collective-permute-done.2.got_left_ref, bf16[4,8,4096]{2,1,0:T(8,128)(2,1)S(1)} %collective-permute-done.3.got_right_ref, ...), custom_call_target="tpu_custom_call" | custom-call | tf_op jit(solution)/shard_map/combine/pallas_call | solution.py:418
  38.0 5.8 %all-to-all-start = ((bf16[4,8,4096]{2,1,0:T(8,128)(2,1)}), bf16[4,8,4096]{2,1,0:T(8,128)(2,1)S(1)}, u32[]{:S(2)}, u32[]{:S(2)}) async-start(bf16[4,8,4096]{2,1,0:T(8,128)(2,1)} %get-tuple-element.30), calls=%async_computation | async-start | bytes 524288 | tf_op jit(solution)/shard_map/all_to_all | solution.py:428
  43.8 3.4 %collective-permute-start.5 = (bf16[48,256]{1,0:T(8,128)(2,1)S(1)}, bf16[48,256]{1,0:T(8,128)(2,1)S(1)}, u32[]{:S(2)}, u32[]{:S(2)}) collective-permute-start(bf16[48,256]{1,0:T(8,128)(2,1)S(1)} %get-tuple-element.31), channel_id=1, source_target_pairs={{0,756},{12,24},{24,12},{36,48},{48,36},{60,72},{72,60},{84,96},{9... | collective-permute-start | bytes 73736 | tf_op jit(solution)/shard_map/ppermute | solution.py:305
  47.3 5.3 %collective-permute-done.5.got_other_ref = bf16[48,256]{1,0:T(8,128)(2,1)S(1)} collective-permute-done((bf16[48,256]{1,0:T(8,128)(2,1)S(1)}, bf16[48,256]{1,0:T(8,128)(2,1)S(1)}, u32[]{:S(2)}, u32[]{:S(2)}) %collective-permute-start.5) | collective-permute-done | bytes 24608 | tf_op jit(solution)/shard_map/ppermute | solution.py:305
  52.5 7.2 %all-to-all-done.heads_ref = bf16[4,8,4096]{2,1,0:T(8,128)(2,1)S(1)} async-done(((bf16[4,8,4096]{2,1,0:T(8,128)(2,1)}), bf16[4,8,4096]{2,1,0:T(8,128)(2,1)S(1)}, u32[]{:S(2)}, u32[]{:S(2)}) %all-to-all-start) | async-done | bytes 262176 | tf_op jit(solution)/shard_map/all_to_all | solution.py:428
  59.7 0.7 %finish.1 = (bf16[4,48,256]{2,1,0:T(8,128)(2,1)}, bf16[2,4,4096]{2,1,0:T(4,128)(2,1)}) custom-call(bf16[4,8,4096]{2,1,0:T(8,128)(2,1)S(1)} %all-to-all-done.heads_ref, bf16[4,48,256]{2,1,0:T(8,128)(2,1)S(1)} %get-tuple-element.29.context_ref, bf16[48,256]{1,0:T(8,128)(2,1)S(1)} %collective-permute-done.4.got_mate_ref, ...), custom_call_target="tpu_custom_call" | custom-call | tf_op jit(solution)/shard_map/finish/pallas_call | solution.py:429
  (1 shorter events, 0.0 us)
Async XLA Ops:
  3.9 14.4 %collective-permute-start = (bf16[48,256]{1,0:T(8,128)(2,1)S(1)}, bf16[48,256]{1,0:T(8,128)(2,1)S(1)}, u32[]{:S(2)}, u32[]{:S(2)}) collective-permute-start(bf16[48,256]{1,0:T(8,128)(2,1)S(1)} %get-tuple-element.24), channel_id=1, source_target_pairs={{0,12},{12,0},{24,36},{36,24},{48,60},{60,48},{72,84},{84,72},{96,... | collective-permute-start | bytes 73736 | tf_op jit(solution)/shard_map/ppermute | solution.py:305
  6.5 11.8 %collective-permute-start.1 = (bf16[48,256]{1,0:T(8,128)(2,1)S(1)}, bf16[48,256]{1,0:T(8,128)(2,1)S(1)}, u32[]{:S(2)}, u32[]{:S(2)}) collective-permute-start(bf16[48,256]{1,0:T(8,128)(2,1)S(1)} %get-tuple-element.25), channel_id=1, source_target_pairs={{0,756},{12,24},{24,12},{36,48},{48,36},{60,72},{72,60},{84,96},{9... | collective-permute-start | bytes 73736 | tf_op jit(solution)/shard_map/ppermute | solution.py:305
  21.0 16.0 %collective-permute-start.2 = (bf16[4,8,4096]{2,1,0:T(8,128)(2,1)S(1)}, bf16[4,8,4096]{2,1,0:T(8,128)(2,1)S(1)}, u32[]{:S(2)}, u32[]{:S(2)}) collective-permute-start(bf16[4,8,4096]{2,1,0:T(8,128)(2,1)S(1)} %get-tuple-element.27), channel_id=1, source_target_pairs={{0,1},{1,2},{2,3},{3,4},{4,5},{5,6},{6,7},{7,8},{8,9},{9,10},{10,1... | collective-permute-start | bytes 786440 | tf_op jit(solution)/shard_map/ppermute | solution.py:407
  23.0 14.3 %collective-permute-start.3 = (bf16[4,8,4096]{2,1,0:T(8,128)(2,1)S(1)}, bf16[4,8,4096]{2,1,0:T(8,128)(2,1)S(1)}, u32[]{:S(2)}, u32[]{:S(2)}) collective-permute-start(bf16[4,8,4096]{2,1,0:T(8,128)(2,1)S(1)} %get-tuple-element.28), channel_id=1, source_target_pairs={{0,11},{1,0},{2,1},{3,2},{4,3},{5,4},{6,5},{7,6},{8,7},{9,8},{10,9... | collective-permute-start | bytes 786440 | tf_op jit(solution)/shard_map/ppermute | solution.py:408
  34.0 3.1 %collective-permute-start.4 = (bf16[48,256]{1,0:T(8,128)(2,1)S(1)}, bf16[48,256]{1,0:T(8,128)(2,1)S(1)}, u32[]{:S(2)}, u32[]{:S(2)}) collective-permute-start(bf16[48,256]{1,0:T(8,128)(2,1)S(1)} %address.1), channel_id=1, source_target_pairs={{0,12},{12,0},{24,36},{36,24},{48,60},{60,48},{72,84},{84,72},{96,... | collective-permute-start | bytes 73736 | tf_op jit(solution)/shard_map/ppermute | solution.py:305
  38.0 21.7 %all-to-all-start = ((bf16[4,8,4096]{2,1,0:T(8,128)(2,1)}), bf16[4,8,4096]{2,1,0:T(8,128)(2,1)S(1)}, u32[]{:S(2)}, u32[]{:S(2)}) async-start(bf16[4,8,4096]{2,1,0:T(8,128)(2,1)} %get-tuple-element.30), calls=%async_computation | async-start | bytes 524288 | tf_op jit(solution)/shard_map/all_to_all | solution.py:428
  43.8 8.7 %collective-permute-start.5 = (bf16[48,256]{1,0:T(8,128)(2,1)S(1)}, bf16[48,256]{1,0:T(8,128)(2,1)S(1)}, u32[]{:S(2)}, u32[]{:S(2)}) collective-permute-start(bf16[48,256]{1,0:T(8,128)(2,1)S(1)} %get-tuple-element.31), channel_id=1, source_target_pairs={{0,756},{12,24},{24,12},{36,48},{48,36},{60,72},{72,60},{84,96},{9... | collective-permute-start | bytes 73736 | tf_op jit(solution)/shard_map/ppermute | solution.py:305

commit v5 on v4

--- a/solution.py
+++ b/solution.py
@@ -30,7 +30,7 @@
     return lax.rem(lax.axis_index("dp"), 2) == 0
 
 
-def prepare(
+def forward(
     chunk,
     inputs_hbm,
     denoiser_hbm,
@@ -44,13 +44,15 @@
     w_key_hbm,
     w_value_hbm,
     shaped_ref,
-    normed_ref,
     w_ref,
+    turned_ref,
     marks_ref,
     own_ref,
-    pay_mate_ref,
-    pay_other_ref,
+    wide_ref,
+    soft_ref,
+    context_ref,
     inputs_v,
+    normed_v,
     span_v,
     mode_v,
     sentinel_v,
@@ -68,7 +70,7 @@
         for i, (source, target) in enumerate(
             (
                 (inputs_hbm, inputs_v),
-                (cotangent_hbm, cotangent_v),
+                (cotangent_hbm.at[pl.ds(0, rows)], cotangent_v),
                 (mode_hbm, mode_v),
                 (sentinel_hbm, sentinel_v),
                 (span_hbm, span_v),
@@ -85,11 +87,6 @@
         copy.start()
     for copy in copies[:8]:
         copy.wait()
-
-    even = is_even()
-    to_right, to_left = cotangent_v[rows + 1], cotangent_v[rows]
-    pay_mate_ref[...] = jnp.where(even, to_right, to_left)
-    pay_other_ref[...] = jnp.where(even, to_left, to_right)
 
     span = [column(span_v[r : r + 1, :]) == 1.0 for r in range(rows)]
     squares = [jnp.zeros((length, 128), F32) for _ in range(rows)]
@@ -112,7 +109,7 @@
     inv_rms = lax.rsqrt(mean + 1e-06)
     for c in range(chunks):
         at = pl.ds(c * chunk, chunk)
-        normed_ref[:, at] = (shaped_ref[:, at].astype(F32) * inv_rms).astype(BF16)
+        normed_v[:, at] = (shaped_ref[:, at].astype(F32) * inv_rms).astype(BF16)
 
     t_at = lax.broadcasted_iota(jnp.int32, (length, 128), 0)
     lane = lax.broadcasted_iota(jnp.int32, (length, 128), 1)
@@ -129,35 +126,20 @@
         marks = jnp.where((lane == 3) & jnp.logical_not(span[r]), 1.0, marks)
         marks = jnp.where((lane == 4) & valid & (move == 0), 1.0, marks)
         marks_ref[here, :] = jnp.where(lane == 5, jnp.maximum(count, 1).astype(F32), marks)
-    for copy in copies[8:]:
-        copy.wait()
-
-
-def forward(
-    chunk,
-    rows,
-    w_ref,
-    normed_ref,
-    marks_ref,
-    wide_ref,
-    soft_ref,
-    context_ref,
-):
-    tokens, width = normed_ref.shape
-    length = tokens // rows
+
+    marks = marks_ref[...]
     head = w_ref.shape[2]
-    totals = []
-    for i in range(3):
-        total = None
-        for c in range(width // chunk):
-            at = pl.ds(c * chunk, chunk)
-            part = dot(normed_ref[:, at], w_ref[i, at, :], ((1,), (0,)))
-            total = part if total is None else total + part
+
+    def project(i):
+        copies[8 + i].wait()
+        total = dot(normed_v[...], w_ref[i], ((1,), (0,)))
         wide_ref[i] = total
-        totals.append(total.astype(BF16))
-    query, key, value = totals
-
-    marks = marks_ref[...]
+        if i < turned_ref.shape[0]:
+            turned_ref[i] = w_ref[i].T
+        return total.astype(BF16)
+
+    query = project(0)
+    key = project(1)
     factor = 1.0 / math.sqrt(head)
     q_at = lax.broadcasted_iota(jnp.int32, (tokens, tokens), 0)
     k_at = lax.broadcasted_iota(jnp.int32, (tokens, tokens), 1)
@@ -170,7 +152,7 @@
     exp_scores = jnp.exp(scores - jnp.max(scores, axis=1, keepdims=True))
     soft = exp_scores / jnp.sum(exp_scores, axis=1, keepdims=True)
     soft_ref[...] = soft
-    context = dot(soft.astype(BF16), value, ((1,), (0,)))
+    context = dot(soft.astype(BF16), project(2), ((1,), (0,)))
 
     def only(lane):
         return jnp.where(marks[:, lane : lane + 1] == 1.0, context, 0.0)
@@ -202,7 +184,7 @@
     return jnp.where(from_at == want, 1.0, 0.0).astype(BF16)
 
 
-def emit(chunk, rows, gradients, w_ref, shaped_ref, inv_rms, inner, keep, out_refs):
+def emit(chunk, rows, gradients, w_ref, turned_ref, shaped_ref, inv_rms, inner, keep, out_refs):
     tokens, width = shaped_ref.shape
     pieces, piece, _ = out_refs[0].shape
     scale = jnp.where(keep, inv_rms, 0.0)
@@ -212,7 +194,10 @@
         at = pl.ds(c * chunk, chunk)
         total = None
         for i in range(3):
-            part = dot(gradients[i], w_ref[i, at, :], ((1,), (1,)))
+            if i < turned_ref.shape[0]:
+                part = dot(gradients[i], turned_ref[i, :, at], ((1,), (0,)))
+            else:
+                part = dot(gradients[i], w_ref[i, at, :], ((1,), (1,)))
             total = part if total is None else total + part
         part = ((total - shaped_ref[:, at].astype(F32) * back) * scale).astype(BF16)
         part = dot(order, part, ((1,), (0,))).astype(BF16)
@@ -225,22 +210,23 @@
 def backward(
     chunk,
     w_ref,
+    turned_ref,
     shaped_ref,
     marks_ref,
     wide_ref,
     soft_ref,
     own_ref,
+    got_other_ref,
     got_mate_ref,
-    got_other_ref,
     *out_refs,
 ):
     tokens, width = shaped_ref.shape
-    rows = tokens // got_mate_ref.shape[0]
+    rows = tokens // got_mate_ref.shape[1]
     head = w_ref.shape[2]
 
     even = is_even()
-    from_right = jnp.where(even, got_mate_ref[...], got_other_ref[...]).astype(F32)
-    from_left = jnp.where(even, got_other_ref[...], got_mate_ref[...]).astype(F32)
+    from_right = jnp.where(even, got_mate_ref[rows], got_other_ref[rows]).astype(F32)
+    from_left = jnp.where(even, got_other_ref[rows + 1], got_mate_ref[rows + 1]).astype(F32)
     marks = marks_ref[...]
     inv_rms = marks[:, 0:1]
     grad_out = jnp.where(
@@ -265,7 +251,7 @@
     gradients = (grad_query, grad_key, grad_value)
     inner = sum(gradients[i].astype(F32) * wide_ref[i] for i in range(3))
     inner = jnp.sum(inner, axis=1, keepdims=True) * (1.0 / width)
-    emit(chunk, rows, gradients, w_ref, shaped_ref, inv_rms, inner, marks[:, 3:4] == 1.0, out_refs)
+    emit(chunk, rows, gradients, w_ref, turned_ref, shaped_ref, inv_rms, inner, marks[:, 3:4] == 1.0, out_refs)
 
 
 def combine(
@@ -335,32 +321,36 @@
         return jax.ShapeDtypeStruct(dims, dtype)
 
     slot = shape((length, head), BF16)
-    shaped, normed, w_all, marks, own, pay_mate, pay_other = pl.pallas_call(
-        lambda *refs: prepare(chunk, *refs),
+    cotangent_mate = exchange(cotangent, mates)
+    cotangent_other = exchange(cotangent, others)
+    shaped, w_all, turned, marks, own, wide, soft, context = pl.pallas_call(
+        lambda *refs: forward(chunk, *refs),
         out_shape=(
             shape((tokens, width), BF16),
-            shape((tokens, width), BF16),
             shape((3, width, head), BF16),
+            shape((2, head, width), BF16),
             shape((tokens, 128), F32),
             shape((tokens, head), BF16),
-            slot,
-            slot,
+            shape((3, tokens, head), F32),
+            shape((tokens, tokens), F32),
+            shape((2 * rows, length, head), BF16),
         ),
         in_specs=[hbm] * 11,
-        out_specs=[vmem] * 7,
+        out_specs=[vmem] * 8,
         scratch_shapes=[
             pltpu.VMEM((rows, length, width), BF16),
+            pltpu.VMEM((tokens, width), BF16),
             pltpu.VMEM(span_mask.shape, jnp.int32),
             pltpu.VMEM(mode_table.shape, BF16),
             pltpu.VMEM((width,), BF16),
-            pltpu.VMEM(cotangent.shape, BF16),
+            pltpu.VMEM((rows, length, head), BF16),
             pltpu.SMEM((rows,), jnp.int32),
             pltpu.SMEM((rows,), jnp.int32),
             pltpu.SMEM((rows,), jnp.int32),
             pltpu.SemaphoreType.DMA((11,)),
         ],
         compiler_params=params,
-        name="prepare",
+        name="forward",
     )(
         *(
             pltpu.with_memory_space_constraint(array, pltpu.HBM)
@@ -379,31 +369,16 @@
             )
         )
     )
-    cotangent_other = exchange(pay_other, others)
-    cotangent_mate = exchange(pay_mate, mates)
-
-    wide, soft, context = pl.pallas_call(
-        lambda *refs: forward(chunk, rows, *refs),
-        out_shape=(
-            shape((3, tokens, head), F32),
-            shape((tokens, tokens), F32),
-            shape((2 * rows, length, head), BF16),
-        ),
-        in_specs=[vmem] * 3,
-        out_specs=[vmem] * 3,
-        compiler_params=params,
-        name="forward",
-    )(w_all, normed, marks)
 
     part = shape((members // WINDOW, rows * seg, width), BF16)
     keep, to_right, to_left = pl.pallas_call(
         lambda *refs: backward(width, *refs),
         out_shape=(part, part, part),
-        in_specs=[vmem] * 8,
+        in_specs=[vmem] * 9,
         out_specs=[vmem] * 3,
         compiler_params=params,
         name="backward",
-    )(w_all, shaped, marks, wide, soft, own, cotangent_mate, cotangent_other)
+    )(w_all, turned, shaped, marks, wide, soft, own, cotangent_other, cotangent_mate)
     from_left = lax.ppermute(to_right, "mp", [(m, (m + 1) % members) for m in range(members)])
     from_right = lax.ppermute(to_left, "mp", [(m, (m - 1) % members) for m in range(members)])
     pay_mate = pl.pallas_call(

time: 60.8 us -> 59.9 us (0.985)
  the two profiles are of different devices: /device:TPU:63 before, /device:TPU:60 now
where the time goes in v5:
time: 59.9 us; the launch traced here: 59.5 us
  starting transfers between devices  32.3 us (54%)
  waiting for transfers between devices  18.4 us (31%)
  Pallas kernels  8.06 us (13%)
  between operations  0.72 us (1%)
    ppermute x1, starting transfers between devices, shards(): lax.ppermute(to_left, 'mp', [(m, (m - 1) % members) for m in range(member...  12.2 us
    all_to_all x1, waiting for transfers between devices, shards(): heads = lax.all_to_all(windows, 'mp', 0, 0, axis_index_groups=spread)  11.1 us
    ppermute x4, starting transfers between devices, exchange(): return lax.ppermute(array, 'dp', pairs)  9.77 us
    all_to_all x1, starting transfers between devices, shards(): heads = lax.all_to_all(windows, 'mp', 0, 0, axis_index_groups=spread)  6.07 us
    pallas_call x1, Pallas kernels, shards(): pl.pallas_call(lambda *refs: forward(chunk, *refs), out_shape=(shape((tok...  4.41 us
    ppermute x1, starting transfers between devices, shards(): lax.ppermute(to_right, 'mp', [(m, (m + 1) % members) for m in range(membe...  4.29 us
    ppermute x4, waiting for transfers between devices, exchange(): return lax.ppermute(array, 'dp', pairs)  4.05 us
    pallas_call x1, Pallas kernels, shards(): pl.pallas_call(lambda *refs: backward(width, *refs), out_shape=(part, par...  2.14 us
  transfers between devices with their start and end apart: 7, of which 5 were waited for; matrix products, arithmetic and copies ran while one was open for 0% of the time, Pallas kernels for 7%

profile of v5, /device:TPU:60, one launch (start us, length us, event | category | flops | bytes accessed | tf_op | source)
XLA Modules:
  0.0 59.5 jit_solution(9559970802998635250)
XLA Ops:
  0.6 1.9 %collective-permute-start.1 = (bf16[4,48,256]{2,1,0:T(8,128)(2,1)}, bf16[4,48,256]{2,1,0:T(8,128)(2,1)S(1)}, u32[]{:S(2)}, u32[]{:S(2)}) collective-permute-start(bf16[4,48,256]{2,1,0:T(8,128)(2,1)} %refs_7_.1), channel_id=1, source_target_pairs={{0,12},{12,0},{24,36},{36,24},{48,60},{60,48},{72,84},{84,72},{96,... | collective-permute-start | bytes 294920 | tf_op jit(solution)/shard_map/ppermute | solution.py:291
  2.6 3.4 %collective-permute-start = (bf16[4,48,256]{2,1,0:T(8,128)(2,1)}, bf16[4,48,256]{2,1,0:T(8,128)(2,1)S(1)}, u32[]{:S(2)}, u32[]{:S(2)}) collective-permute-start(bf16[4,48,256]{2,1,0:T(8,128)(2,1)} %refs_7_.1), channel_id=1, source_target_pairs={{0,756},{12,24},{24,12},{36,48},{48,36},{60,72},{72,60},{84,96},{9... | collective-permute-start | bytes 294920 | tf_op jit(solution)/shard_map/ppermute | solution.py:291
  5.9 4.4 %forward.1 = (bf16[96,4096]{1,0:T(8,128)(2,1)S(1)}, bf16[3,4096,256]{2,1,0:T(8,128)(2,1)S(1)}, bf16[2,256,4096]{2,1,0:T(8,128)(2,1)S(1)}, f32[96,128]{1,0:T(8,12...) custom-call(bf16[2,48,4096]{2,1,0:T(8,128)(2,1)} %refs_0_.1, ...), custom_call_target="tpu_custom_call" | custom-call | tf_op jit(solution)/shard_map/forward/pallas_call | solution.py:326
  10.3 0.0 collective-permute-done.1.refs_8_
  10.4 0.0 collective-permute-done.refs_7_
  10.4 2.1 %backward.1 = (bf16[4,8,4096]{2,1,0:T(8,128)(2,1)S(1)}, bf16[4,8,4096]{2,1,0:T(8,128)(2,1)S(1)}, bf16[4,8,4096]{2,1,0:T(8,128)(2,1)S(1)}) custom-call(bf16[3,4096,256]{2,1,0:T(8,128)(2,1)S(1)} %get-tuple-element.15.refs_0_, bf16[2,256,4096]{2,1,0:T(8,128)(2,1)S(1)} %get-tuple-element.16.refs_1_, bf16[96,4096]{1,0:T(8,128)(2,1)S(1)} %get-tuple-element.17.refs_2_, ...), custom_call_target="tpu_custom_call" | custom-call | tf_op jit(solution)/shard_map/backward/pallas_call | solution.py:374
  12.5 4.3 %collective-permute-start.2 = (bf16[4,8,4096]{2,1,0:T(8,128)(2,1)S(1)}, bf16[4,8,4096]{2,1,0:T(8,128)(2,1)S(1)}, u32[]{:S(2)}, u32[]{:S(2)}) collective-permute-start(bf16[4,8,4096]{2,1,0:T(8,128)(2,1)S(1)} %get-tuple-element.23), channel_id=1, source_target_pairs={{0,1},{1,2},{2,3},{3,4},{4,5},{5,6},{6,7},{7,8},{8,9},{9,10},{10,1... | collective-permute-start | bytes 786440 | tf_op jit(solution)/shard_map/ppermute | solution.py:382
  16.8 12.2 %collective-permute-start.3 = (bf16[4,8,4096]{2,1,0:T(8,128)(2,1)S(1)}, bf16[4,8,4096]{2,1,0:T(8,128)(2,1)S(1)}, u32[]{:S(2)}, u32[]{:S(2)}) collective-permute-start(bf16[4,8,4096]{2,1,0:T(8,128)(2,1)S(1)} %get-tuple-element.24), channel_id=1, source_target_pairs={{0,11},{1,0},{2,1},{3,2},{4,3},{5,4},{6,5},{7,6},{8,7},{9,8},{10,9... | collective-permute-start | bytes 786440 | tf_op jit(solution)/shard_map/ppermute | solution.py:383
  29.1 2.6 %collective-permute-start.4 = (bf16[48,256]{1,0:T(8,128)(2,1)S(1)}, bf16[48,256]{1,0:T(8,128)(2,1)S(1)}, u32[]{:S(2)}, u32[]{:S(2)}) collective-permute-start(bf16[48,256]{1,0:T(8,128)(2,1)S(1)} %address.1), channel_id=1, source_target_pairs={{0,12},{12,0},{24,36},{36,24},{48,60},{60,48},{72,84},{84,72},{96,... | collective-permute-start | bytes 73736 | tf_op jit(solution)/shard_map/ppermute | solution.py:291
  31.6 0.8 %collective-permute-done.4.got_mate_ref = bf16[48,256]{1,0:T(8,128)(2,1)S(1)} collective-permute-done((bf16[48,256]{1,0:T(8,128)(2,1)S(1)}, bf16[48,256]{1,0:T(8,128)(2,1)S(1)}, u32[]{:S(2)}, u32[]{:S(2)}) %collective-permute-start.4) | collective-permute-done | bytes 24608 | tf_op jit(solution)/shard_map/ppermute | solution.py:291
  32.5 1.5 %collective-permute-done.2.got_left_ref = bf16[4,8,4096]{2,1,0:T(8,128)(2,1)S(1)} collective-permute-done((bf16[4,8,4096]{2,1,0:T(8,128)(2,1)S(1)}, bf16[4,8,4096]{2,1,0:T(8,128)(2,1)S(1)}, u32[]{:S(2)}, u32[]{:S(2)}) %collective-permute-start.2) | collective-permute-done | bytes 262176 | tf_op jit(solution)/shard_map/ppermute | solution.py:382
  34.0 1.7 %collective-permute-done.3.got_right_ref = bf16[4,8,4096]{2,1,0:T(8,128)(2,1)S(1)} collective-permute-done((bf16[4,8,4096]{2,1,0:T(8,128)(2,1)S(1)}, bf16[4,8,4096]{2,1,0:T(8,128)(2,1)S(1)}, u32[]{:S(2)}, u32[]{:S(2)}) %collective-permute-start.3) | collective-permute-done | bytes 262176 | tf_op jit(solution)/shard_map/ppermute | solution.py:383
  35.7 0.8 %combine.1 = (bf16[4,8,4096]{2,1,0:T(8,128)(2,1)}, bf16[48,256]{1,0:T(8,128)(2,1)S(1)}) custom-call(bf16[4,8,4096]{2,1,0:T(8,128)(2,1)S(1)} %get-tuple-element.22.keep_ref, bf16[4,8,4096]{2,1,0:T(8,128)(2,1)S(1)} %collective-permute-done.2.got_left_ref, bf16[4,8,4096]{2,1,0:T(8,128)(2,1)S(1)} %collective-permute-done.3.got_right_ref, ...), custom_call_target="tpu_custom_call" | custom-call | tf_op jit(solution)/shard_map/combine/pallas_call | solution.py:393
  36.5 6.1 %all-to-all-start = ((bf16[4,8,4096]{2,1,0:T(8,128)(2,1)}), bf16[4,8,4096]{2,1,0:T(8,128)(2,1)S(1)}, u32[]{:S(2)}, u32[]{:S(2)}) async-start(bf16[4,8,4096]{2,1,0:T(8,128)(2,1)} %get-tuple-element.26), calls=%async_computation | async-start | bytes 524288 | tf_op jit(solution)/shard_map/all_to_all | solution.py:403
  42.6 1.9 %collective-permute-start.5 = (bf16[48,256]{1,0:T(8,128)(2,1)S(1)}, bf16[48,256]{1,0:T(8,128)(2,1)S(1)}, u32[]{:S(2)}, u32[]{:S(2)}) collective-permute-start(bf16[48,256]{1,0:T(8,128)(2,1)S(1)} %get-tuple-element.27), channel_id=1, source_target_pairs={{0,756},{12,24},{24,12},{36,48},{48,36},{60,72},{72,60},{84,96},{9... | collective-permute-start | bytes 73736 | tf_op jit(solution)/shard_map/ppermute | solution.py:291
  44.5 3.2 %collective-permute-done.5.got_other_ref = bf16[48,256]{1,0:T(8,128)(2,1)S(1)} collective-permute-done((bf16[48,256]{1,0:T(8,128)(2,1)S(1)}, bf16[48,256]{1,0:T(8,128)(2,1)S(1)}, u32[]{:S(2)}, u32[]{:S(2)}) %collective-permute-start.5) | collective-permute-done | bytes 24608 | tf_op jit(solution)/shard_map/ppermute | solution.py:291
  47.7 11.1 %all-to-all-done.heads_ref = bf16[4,8,4096]{2,1,0:T(8,128)(2,1)S(1)} async-done(((bf16[4,8,4096]{2,1,0:T(8,128)(2,1)}), bf16[4,8,4096]{2,1,0:T(8,128)(2,1)S(1)}, u32[]{:S(2)}, u32[]{:S(2)}) %all-to-all-start) | async-done | bytes 262176 | tf_op jit(solution)/shard_map/all_to_all | solution.py:403
  58.8 0.7 %finish.1 = (bf16[4,48,256]{2,1,0:T(8,128)(2,1)}, bf16[2,4,4096]{2,1,0:T(4,128)(2,1)}) custom-call(bf16[4,8,4096]{2,1,0:T(8,128)(2,1)S(1)} %all-to-all-done.heads_ref, bf16[4,48,256]{2,1,0:T(8,128)(2,1)S(1)} %get-tuple-element.25.context_ref, bf16[48,256]{1,0:T(8,128)(2,1)S(1)} %collective-permute-done.4.got_mate_ref, ...), custom_call_target="tpu_custom_call" | custom-call | tf_op jit(solution)/shard_map/finish/pallas_call | solution.py:404
  (1 shorter events, 0.0 us)
Async XLA Ops:
  0.6 9.7 %collective-permute-start.1 = (bf16[4,48,256]{2,1,0:T(8,128)(2,1)}, bf16[4,48,256]{2,1,0:T(8,128)(2,1)S(1)}, u32[]{:S(2)}, u32[]{:S(2)}) collective-permute-start(bf16[4,48,256]{2,1,0:T(8,128)(2,1)} %refs_7_.1), channel_id=1, source_target_pairs={{0,12},{12,0},{24,36},{36,24},{48,60},{60,48},{72,84},{84,72},{96,... | collective-permute-start | bytes 294920 | tf_op jit(solution)/shard_map/ppermute | solution.py:291
  2.6 7.8 %collective-permute-start = (bf16[4,48,256]{2,1,0:T(8,128)(2,1)}, bf16[4,48,256]{2,1,0:T(8,128)(2,1)S(1)}, u32[]{:S(2)}, u32[]{:S(2)}) collective-permute-start(bf16[4,48,256]{2,1,0:T(8,128)(2,1)} %refs_7_.1), channel_id=1, source_target_pairs={{0,756},{12,24},{24,12},{36,48},{48,36},{60,72},{72,60},{84,96},{9... | collective-permute-start | bytes 294920 | tf_op jit(solution)/shard_map/ppermute | solution.py:291
  12.5 21.5 %collective-permute-start.2 = (bf16[4,8,4096]{2,1,0:T(8,128)(2,1)S(1)}, bf16[4,8,4096]{2,1,0:T(8,128)(2,1)S(1)}, u32[]{:S(2)}, u32[]{:S(2)}) collective-permute-start(bf16[4,8,4096]{2,1,0:T(8,128)(2,1)S(1)} %get-tuple-element.23), channel_id=1, source_target_pairs={{0,1},{1,2},{2,3},{3,4},{4,5},{5,6},{6,7},{7,8},{8,9},{9,10},{10,1... | collective-permute-start | bytes 786440 | tf_op jit(solution)/shard_map/ppermute | solution.py:382
  16.8 18.9 %collective-permute-start.3 = (bf16[4,8,4096]{2,1,0:T(8,128)(2,1)S(1)}, bf16[4,8,4096]{2,1,0:T(8,128)(2,1)S(1)}, u32[]{:S(2)}, u32[]{:S(2)}) collective-permute-start(bf16[4,8,4096]{2,1,0:T(8,128)(2,1)S(1)} %get-tuple-element.24), channel_id=1, source_target_pairs={{0,11},{1,0},{2,1},{3,2},{4,3},{5,4},{6,5},{7,6},{8,7},{9,8},{10,9... | collective-permute-start | bytes 786440 | tf_op jit(solution)/shard_map/ppermute | solution.py:383
  29.1 3.4 %collective-permute-start.4 = (bf16[48,256]{1,0:T(8,128)(2,1)S(1)}, bf16[48,256]{1,0:T(8,128)(2,1)S(1)}, u32[]{:S(2)}, u32[]{:S(2)}) collective-permute-start(bf16[48,256]{1,0:T(8,128)(2,1)S(1)} %address.1), channel_id=1, source_target_pairs={{0,12},{12,0},{24,36},{36,24},{48,60},{60,48},{72,84},{84,72},{96,... | collective-permute-start | bytes 73736 | tf_op jit(solution)/shard_map/ppermute | solution.py:291
  36.5 22.3 %all-to-all-start = ((bf16[4,8,4096]{2,1,0:T(8,128)(2,1)}), bf16[4,8,4096]{2,1,0:T(8,128)(2,1)S(1)}, u32[]{:S(2)}, u32[]{:S(2)}) async-start(bf16[4,8,4096]{2,1,0:T(8,128)(2,1)} %get-tuple-element.26), calls=%async_computation | async-start | bytes 524288 | tf_op jit(solution)/shard_map/all_to_all | solution.py:403
  42.6 5.1 %collective-permute-start.5 = (bf16[48,256]{1,0:T(8,128)(2,1)S(1)}, bf16[48,256]{1,0:T(8,128)(2,1)S(1)}, u32[]{:S(2)}, u32[]{:S(2)}) collective-permute-start(bf16[48,256]{1,0:T(8,128)(2,1)S(1)} %get-tuple-element.27), channel_id=1, source_target_pairs={{0,756},{12,24},{24,12},{36,48},{48,36},{60,72},{72,60},{84,96},{9... | collective-permute-start | bytes 73736 | tf_op jit(solution)/shard_map/ppermute | solution.py:291

commit v6 on v5

--- a/solution.py
+++ b/solution.py
@@ -44,7 +44,6 @@
     w_key_hbm,
     w_value_hbm,
     shaped_ref,
-    w_ref,
     turned_ref,
     marks_ref,
     own_ref,
@@ -53,6 +52,7 @@
     context_ref,
     inputs_v,
     normed_v,
+    w_v,
     span_v,
     mode_v,
     sentinel_v,
@@ -77,9 +77,9 @@
                 (denoiser_hbm, denoiser_s),
                 (lengths_hbm, lengths_s),
                 (move_hbm, move_s),
-                (w_query_hbm, w_ref.at[0]),
-                (w_key_hbm, w_ref.at[1]),
-                (w_value_hbm, w_ref.at[2]),
+                (w_query_hbm, w_v.at[0]),
+                (w_key_hbm, w_v.at[1]),
+                (w_value_hbm, w_v.at[2]),
             )
         )
     ]
@@ -128,14 +128,13 @@
         marks_ref[here, :] = jnp.where(lane == 5, jnp.maximum(count, 1).astype(F32), marks)
 
     marks = marks_ref[...]
-    head = w_ref.shape[2]
+    head = w_v.shape[2]
 
     def project(i):
         copies[8 + i].wait()
-        total = dot(normed_v[...], w_ref[i], ((1,), (0,)))
+        total = dot(normed_v[...], w_v[i], ((1,), (0,)))
         wide_ref[i] = total
-        if i < turned_ref.shape[0]:
-            turned_ref[i] = w_ref[i].T
+        turned_ref[i] = w_v[i].T
         return total.astype(BF16)
 
     query = project(0)
@@ -184,7 +183,7 @@
     return jnp.where(from_at == want, 1.0, 0.0).astype(BF16)
 
 
-def emit(chunk, rows, gradients, w_ref, turned_ref, shaped_ref, inv_rms, inner, keep, out_refs):
+def emit(chunk, rows, gradients, turned_ref, shaped_ref, inv_rms, inner, keep, out_refs):
     tokens, width = shaped_ref.shape
     pieces, piece, _ = out_refs[0].shape
     scale = jnp.where(keep, inv_rms, 0.0)
@@ -194,22 +193,18 @@
         at = pl.ds(c * chunk, chunk)
         total = None
         for i in range(3):
-            if i < turned_ref.shape[0]:
-                part = dot(gradients[i], turned_ref[i, :, at], ((1,), (0,)))
-            else:
-                part = dot(gradients[i], w_ref[i, at, :], ((1,), (1,)))
+            part = dot(gradients[i], turned_ref[i, :, at], ((1,), (0,)))
             total = part if total is None else total + part
         part = ((total - shaped_ref[:, at].astype(F32) * back) * scale).astype(BF16)
-        part = dot(order, part, ((1,), (0,))).astype(BF16)
+        part = dot(order, part, ((1,), (0,)))
         for s in range(WINDOW):
             for j in range(pieces):
                 low = (s * pieces + j) * piece
-                out_refs[s][j, :, at] = part[low : low + piece]
+                out_refs[s][j, :, at] = part[low : low + piece].astype(BF16)
 
 
 def backward(
     chunk,
-    w_ref,
     turned_ref,
     shaped_ref,
     marks_ref,
@@ -222,7 +217,7 @@
 ):
     tokens, width = shaped_ref.shape
     rows = tokens // got_mate_ref.shape[1]
-    head = w_ref.shape[2]
+    head = turned_ref.shape[1]
 
     even = is_even()
     from_right = jnp.where(even, got_mate_ref[rows], got_other_ref[rows]).astype(F32)
@@ -251,7 +246,7 @@
     gradients = (grad_query, grad_key, grad_value)
     inner = sum(gradients[i].astype(F32) * wide_ref[i] for i in range(3))
     inner = jnp.sum(inner, axis=1, keepdims=True) * (1.0 / width)
-    emit(chunk, rows, gradients, w_ref, turned_ref, shaped_ref, inv_rms, inner, marks[:, 3:4] == 1.0, out_refs)
+    emit(chunk, rows, gradients, turned_ref, shaped_ref, inv_rms, inner, marks[:, 3:4] == 1.0, out_refs)
 
 
 def combine(
@@ -323,12 +318,11 @@
     slot = shape((length, head), BF16)
     cotangent_mate = exchange(cotangent, mates)
     cotangent_other = exchange(cotangent, others)
-    shaped, w_all, turned, marks, own, wide, soft, context = pl.pallas_call(
+    shaped, turned, marks, own, wide, soft, context = pl.pallas_call(
         lambda *refs: forward(chunk, *refs),
         out_shape=(
             shape((tokens, width), BF16),
-            shape((3, width, head), BF16),
-            shape((2, head, width), BF16),
+            shape((3, head, width), BF16),
             shape((tokens, 128), F32),
             shape((tokens, head), BF16),
             shape((3, tokens, head), F32),
@@ -336,10 +330,11 @@
             shape((2 * rows, length, head), BF16),
         ),
         in_specs=[hbm] * 11,
-        out_specs=[vmem] * 8,
+        out_specs=[vmem] * 7,
         scratch_shapes=[
             pltpu.VMEM((rows, length, width), BF16),
             pltpu.VMEM((tokens, width), BF16),
+            pltpu.VMEM((3, width, head), BF16),
             pltpu.VMEM(span_mask.shape, jnp.int32),
             pltpu.VMEM(mode_table.shape, BF16),
             pltpu.VMEM((width,), BF16),
@@ -374,11 +369,11 @@
     keep, to_right, to_left = pl.pallas_call(
         lambda *refs: backward(width, *refs),
         out_shape=(part, part, part),
-        in_specs=[vmem] * 9,
+        in_specs=[vmem] * 8,
         out_specs=[vmem] * 3,
         compiler_params=params,
         name="backward",
-    )(w_all, turned, shaped, marks, wide, soft, own, cotangent_other, cotangent_mate)
+    )(turned, shaped, marks, wide, soft, own, cotangent_other, cotangent_mate)
     from_left = lax.ppermute(to_right, "mp", [(m, (m + 1) % members) for m in range(members)])
     from_right = lax.ppermute(to_left, "mp", [(m, (m - 1) % members) for m in range(members)])
     pay_mate = pl.pallas_call(

time: 59.9 us -> 59.6 us (level)
  transfers between devices with their start and end apart: 7 -> 7, of which waited for: 5 -> 5; matrix products, arithmetic and copies ran while one was open for 0% -> 0% of each run, Pallas kernels for 7% -> 8%
where the time goes in v6:
time: 59.6 us; the launch traced here: 59.2 us
  starting transfers between devices  32.3 us (54%)
  waiting for transfers between devices  18.4 us (31%)
  Pallas kernels  7.84 us (13%)
  between operations  0.72 us (1%)
    ppermute x1, starting transfers between devices, shards(): lax.ppermute(to_left, 'mp', [(m, (m - 1) % members) for m in range(member...  12.2 us
    all_to_all x1, waiting for transfers between devices, shards(): heads = lax.all_to_all(windows, 'mp', 0, 0, axis_index_groups=spread)  11.1 us
    ppermute x4, starting transfers between devices, exchange(): return lax.ppermute(array, 'dp', pairs)  9.73 us
    all_to_all x1, starting transfers between devices, shards(): heads = lax.all_to_all(windows, 'mp', 0, 0, axis_index_groups=spread)  6.07 us
    pallas_call x1, Pallas kernels, shards(): pl.pallas_call(lambda *refs: forward(chunk, *refs), out_shape=(shape((tok...  4.42 us
    ppermute x1, starting transfers between devices, shards(): lax.ppermute(to_right, 'mp', [(m, (m + 1) % members) for m in range(membe...  4.29 us
    ppermute x4, waiting for transfers between devices, exchange(): return lax.ppermute(array, 'dp', pairs)  4.05 us
    pallas_call x1, Pallas kernels, shards(): pl.pallas_call(lambda *refs: backward(width, *refs), out_shape=(part, par...  1.9 us
  transfers between devices with their start and end apart: 7, of which 5 were waited for; matrix products, arithmetic and copies ran while one was open for 0% of the time, Pallas kernels for 8%

profile of v6, /device:TPU:60, one launch (start us, length us, event | category | flops | bytes accessed | tf_op | source)
XLA Modules:
  0.0 59.2 jit_solution(8912938521300631043)
XLA Ops:
  0.6 1.9 %collective-permute-start.1 = (bf16[4,48,256]{2,1,0:T(8,128)(2,1)}, bf16[4,48,256]{2,1,0:T(8,128)(2,1)S(1)}, u32[]{:S(2)}, u32[]{:S(2)}) collective-permute-start(bf16[4,48,256]{2,1,0:T(8,128)(2,1)} %refs_7_.1), channel_id=1, source_target_pairs={{0,12},{12,0},{24,36},{36,24},{48,60},{60,48},{72,84},{84,72},{96,... | collective-permute-start | bytes 294920 | tf_op jit(solution)/shard_map/ppermute | solution.py:286
  2.6 3.4 %collective-permute-start = (bf16[4,48,256]{2,1,0:T(8,128)(2,1)}, bf16[4,48,256]{2,1,0:T(8,128)(2,1)S(1)}, u32[]{:S(2)}, u32[]{:S(2)}) collective-permute-start(bf16[4,48,256]{2,1,0:T(8,128)(2,1)} %refs_7_.1), channel_id=1, source_target_pairs={{0,756},{12,24},{24,12},{36,48},{48,36},{60,72},{72,60},{84,96},{9... | collective-permute-start | bytes 294920 | tf_op jit(solution)/shard_map/ppermute | solution.py:286
  5.9 4.4 %forward.1 = (bf16[96,4096]{1,0:T(8,128)(2,1)S(1)}, bf16[3,256,4096]{2,1,0:T(8,128)(2,1)S(1)}, f32[96,128]{1,0:T(8,128)S(1)}, bf16[96,256]{1,0:T(8,128)(2,1)S(1)...) custom-call(bf16[2,48,4096]{2,1,0:T(8,128)(2,1)} %refs_0_.1, s32[2]{0:T(128)} %refs_1_.1, ...), custom_call_target="tpu_custom_call" | custom-call | tf_op jit(solution)/shard_map/forward/pallas_call | solution.py:321
  10.4 0.0 collective-permute-done.1.refs_7_
  10.4 0.0 collective-permute-done.refs_6_
  10.4 1.9 %backward.1 = (bf16[4,8,4096]{2,1,0:T(8,128)(2,1)S(1)}, bf16[4,8,4096]{2,1,0:T(8,128)(2,1)S(1)}, bf16[4,8,4096]{2,1,0:T(8,128)(2,1)S(1)}) custom-call(bf16[3,256,4096]{2,1,0:T(8,128)(2,1)S(1)} %get-tuple-element.14.refs_0_, bf16[96,4096]{1,0:T(8,128)(2,1)S(1)} %get-tuple-element.15.refs_1_, f32[96,128]{1,0:T(8,128)S(1)} %get-tuple-element.16.refs_2_, ...), custom_call_target="tpu_custom_call" | custom-call | tf_op jit(solution)/shard_map/backward/pallas_call | solution.py:369
  12.3 4.3 %collective-permute-start.2 = (bf16[4,8,4096]{2,1,0:T(8,128)(2,1)S(1)}, bf16[4,8,4096]{2,1,0:T(8,128)(2,1)S(1)}, u32[]{:S(2)}, u32[]{:S(2)}) collective-permute-start(bf16[4,8,4096]{2,1,0:T(8,128)(2,1)S(1)} %get-tuple-element.21), channel_id=1, source_target_pairs={{0,1},{1,2},{2,3},{3,4},{4,5},{5,6},{6,7},{7,8},{8,9},{9,10},{10,1... | collective-permute-start | bytes 786440 | tf_op jit(solution)/shard_map/ppermute | solution.py:377
  16.6 12.2 %collective-permute-start.3 = (bf16[4,8,4096]{2,1,0:T(8,128)(2,1)S(1)}, bf16[4,8,4096]{2,1,0:T(8,128)(2,1)S(1)}, u32[]{:S(2)}, u32[]{:S(2)}) collective-permute-start(bf16[4,8,4096]{2,1,0:T(8,128)(2,1)S(1)} %get-tuple-element.22), channel_id=1, source_target_pairs={{0,11},{1,0},{2,1},{3,2},{4,3},{5,4},{6,5},{7,6},{8,7},{9,8},{10,9... | collective-permute-start | bytes 786440 | tf_op jit(solution)/shard_map/ppermute | solution.py:378
  28.9 2.5 %collective-permute-start.4 = (bf16[48,256]{1,0:T(8,128)(2,1)S(1)}, bf16[48,256]{1,0:T(8,128)(2,1)S(1)}, u32[]{:S(2)}, u32[]{:S(2)}) collective-permute-start(bf16[48,256]{1,0:T(8,128)(2,1)S(1)} %address.1), channel_id=1, source_target_pairs={{0,12},{12,0},{24,36},{36,24},{48,60},{60,48},{72,84},{84,72},{96,... | collective-permute-start | bytes 73736 | tf_op jit(solution)/shard_map/ppermute | solution.py:286
  31.4 0.8 %collective-permute-done.4.got_mate_ref = bf16[48,256]{1,0:T(8,128)(2,1)S(1)} collective-permute-done((bf16[48,256]{1,0:T(8,128)(2,1)S(1)}, bf16[48,256]{1,0:T(8,128)(2,1)S(1)}, u32[]{:S(2)}, u32[]{:S(2)}) %collective-permute-start.4) | collective-permute-done | bytes 24608 | tf_op jit(solution)/shard_map/ppermute | solution.py:286
  32.2 1.6 %collective-permute-done.2.got_left_ref = bf16[4,8,4096]{2,1,0:T(8,128)(2,1)S(1)} collective-permute-done((bf16[4,8,4096]{2,1,0:T(8,128)(2,1)S(1)}, bf16[4,8,4096]{2,1,0:T(8,128)(2,1)S(1)}, u32[]{:S(2)}, u32[]{:S(2)}) %collective-permute-start.2) | collective-permute-done | bytes 262176 | tf_op jit(solution)/shard_map/ppermute | solution.py:377
  33.8 1.7 %collective-permute-done.3.got_right_ref = bf16[4,8,4096]{2,1,0:T(8,128)(2,1)S(1)} collective-permute-done((bf16[4,8,4096]{2,1,0:T(8,128)(2,1)S(1)}, bf16[4,8,4096]{2,1,0:T(8,128)(2,1)S(1)}, u32[]{:S(2)}, u32[]{:S(2)}) %collective-permute-start.3) | collective-permute-done | bytes 262176 | tf_op jit(solution)/shard_map/ppermute | solution.py:378
  35.5 0.8 %combine.1 = (bf16[4,8,4096]{2,1,0:T(8,128)(2,1)}, bf16[48,256]{1,0:T(8,128)(2,1)S(1)}) custom-call(bf16[4,8,4096]{2,1,0:T(8,128)(2,1)S(1)} %get-tuple-element.20.keep_ref, bf16[4,8,4096]{2,1,0:T(8,128)(2,1)S(1)} %collective-permute-done.2.got_left_ref, bf16[4,8,4096]{2,1,0:T(8,128)(2,1)S(1)} %collective-permute-done.3.got_right_ref, ...), custom_call_target="tpu_custom_call" | custom-call | tf_op jit(solution)/shard_map/combine/pallas_call | solution.py:388
  36.3 6.1 %all-to-all-start = ((bf16[4,8,4096]{2,1,0:T(8,128)(2,1)}), bf16[4,8,4096]{2,1,0:T(8,128)(2,1)S(1)}, u32[]{:S(2)}, u32[]{:S(2)}) async-start(bf16[4,8,4096]{2,1,0:T(8,128)(2,1)} %get-tuple-element.24), calls=%async_computation | async-start | bytes 524288 | tf_op jit(solution)/shard_map/all_to_all | solution.py:398
  42.4 1.9 %collective-permute-start.5 = (bf16[48,256]{1,0:T(8,128)(2,1)S(1)}, bf16[48,256]{1,0:T(8,128)(2,1)S(1)}, u32[]{:S(2)}, u32[]{:S(2)}) collective-permute-start(bf16[48,256]{1,0:T(8,128)(2,1)S(1)} %get-tuple-element.25), channel_id=1, source_target_pairs={{0,756},{12,24},{24,12},{36,48},{48,36},{60,72},{72,60},{84,96},{9... | collective-permute-start | bytes 73736 | tf_op jit(solution)/shard_map/ppermute | solution.py:286
  44.3 3.2 %collective-permute-done.5.got_other_ref = bf16[48,256]{1,0:T(8,128)(2,1)S(1)} collective-permute-done((bf16[48,256]{1,0:T(8,128)(2,1)S(1)}, bf16[48,256]{1,0:T(8,128)(2,1)S(1)}, u32[]{:S(2)}, u32[]{:S(2)}) %collective-permute-start.5) | collective-permute-done | bytes 24608 | tf_op jit(solution)/shard_map/ppermute | solution.py:286
  47.5 11.1 %all-to-all-done.heads_ref = bf16[4,8,4096]{2,1,0:T(8,128)(2,1)S(1)} async-done(((bf16[4,8,4096]{2,1,0:T(8,128)(2,1)}), bf16[4,8,4096]{2,1,0:T(8,128)(2,1)S(1)}, u32[]{:S(2)}, u32[]{:S(2)}) %all-to-all-start) | async-done | bytes 262176 | tf_op jit(solution)/shard_map/all_to_all | solution.py:398
  58.5 0.7 %finish.1 = (bf16[4,48,256]{2,1,0:T(8,128)(2,1)}, bf16[2,4,4096]{2,1,0:T(4,128)(2,1)}) custom-call(bf16[4,8,4096]{2,1,0:T(8,128)(2,1)S(1)} %all-to-all-done.heads_ref, bf16[4,48,256]{2,1,0:T(8,128)(2,1)S(1)} %get-tuple-element.23.context_ref, bf16[48,256]{1,0:T(8,128)(2,1)S(1)} %collective-permute-done.4.got_mate_ref, ...), custom_call_target="tpu_custom_call" | custom-call | tf_op jit(solution)/shard_map/finish/pallas_call | solution.py:399
  (1 shorter events, 0.0 us)
Async XLA Ops:
  0.6 9.7 %collective-permute-start.1 = (bf16[4,48,256]{2,1,0:T(8,128)(2,1)}, bf16[4,48,256]{2,1,0:T(8,128)(2,1)S(1)}, u32[]{:S(2)}, u32[]{:S(2)}) collective-permute-start(bf16[4,48,256]{2,1,0:T(8,128)(2,1)} %refs_7_.1), channel_id=1, source_target_pairs={{0,12},{12,0},{24,36},{36,24},{48,60},{60,48},{72,84},{84,72},{96,... | collective-permute-start | bytes 294920 | tf_op jit(solution)/shard_map/ppermute | solution.py:286
  2.6 7.8 %collective-permute-start = (bf16[4,48,256]{2,1,0:T(8,128)(2,1)}, bf16[4,48,256]{2,1,0:T(8,128)(2,1)S(1)}, u32[]{:S(2)}, u32[]{:S(2)}) collective-permute-start(bf16[4,48,256]{2,1,0:T(8,128)(2,1)} %refs_7_.1), channel_id=1, source_target_pairs={{0,756},{12,24},{24,12},{36,48},{48,36},{60,72},{72,60},{84,96},{9... | collective-permute-start | bytes 294920 | tf_op jit(solution)/shard_map/ppermute | solution.py:286
  12.3 21.5 %collective-permute-start.2 = (bf16[4,8,4096]{2,1,0:T(8,128)(2,1)S(1)}, bf16[4,8,4096]{2,1,0:T(8,128)(2,1)S(1)}, u32[]{:S(2)}, u32[]{:S(2)}) collective-permute-start(bf16[4,8,4096]{2,1,0:T(8,128)(2,1)S(1)} %get-tuple-element.21), channel_id=1, source_target_pairs={{0,1},{1,2},{2,3},{3,4},{4,5},{5,6},{6,7},{7,8},{8,9},{9,10},{10,1... | collective-permute-start | bytes 786440 | tf_op jit(solution)/shard_map/ppermute | solution.py:377
  16.6 18.9 %collective-permute-start.3 = (bf16[4,8,4096]{2,1,0:T(8,128)(2,1)S(1)}, bf16[4,8,4096]{2,1,0:T(8,128)(2,1)S(1)}, u32[]{:S(2)}, u32[]{:S(2)}) collective-permute-start(bf16[4,8,4096]{2,1,0:T(8,128)(2,1)S(1)} %get-tuple-element.22), channel_id=1, source_target_pairs={{0,11},{1,0},{2,1},{3,2},{4,3},{5,4},{6,5},{7,6},{8,7},{9,8},{10,9... | collective-permute-start | bytes 786440 | tf_op jit(solution)/shard_map/ppermute | solution.py:378
  28.9 3.4 %collective-permute-start.4 = (bf16[48,256]{1,0:T(8,128)(2,1)S(1)}, bf16[48,256]{1,0:T(8,128)(2,1)S(1)}, u32[]{:S(2)}, u32[]{:S(2)}) collective-permute-start(bf16[48,256]{1,0:T(8,128)(2,1)S(1)} %address.1), channel_id=1, source_target_pairs={{0,12},{12,0},{24,36},{36,24},{48,60},{60,48},{72,84},{84,72},{96,... | collective-permute-start | bytes 73736 | tf_op jit(solution)/shard_map/ppermute | solution.py:286
  36.3 22.3 %all-to-all-start = ((bf16[4,8,4096]{2,1,0:T(8,128)(2,1)}), bf16[4,8,4096]{2,1,0:T(8,128)(2,1)S(1)}, u32[]{:S(2)}, u32[]{:S(2)}) async-start(bf16[4,8,4096]{2,1,0:T(8,128)(2,1)} %get-tuple-element.24), calls=%async_computation | async-start | bytes 524288 | tf_op jit(solution)/shard_map/all_to_all | solution.py:398
  42.4 5.1 %collective-permute-start.5 = (bf16[48,256]{1,0:T(8,128)(2,1)S(1)}, bf16[48,256]{1,0:T(8,128)(2,1)S(1)}, u32[]{:S(2)}, u32[]{:S(2)}) collective-permute-start(bf16[48,256]{1,0:T(8,128)(2,1)S(1)} %get-tuple-element.25), channel_id=1, source_target_pairs={{0,756},{12,24},{24,12},{36,48},{48,36},{60,72},{72,60},{84,96},{9... | collective-permute-start | bytes 73736 | tf_op jit(solution)/shard_map/ppermute | solution.py:286

commit v7 on v6

--- a/solution.py
+++ b/solution.py
@@ -32,6 +32,7 @@
 
 def forward(
     chunk,
+    members,
     inputs_hbm,
     denoiser_hbm,
     span_hbm,
@@ -43,7 +44,7 @@
     w_query_hbm,
     w_key_hbm,
     w_value_hbm,
-    shaped_ref,
+    ordered_ref,
     turned_ref,
     marks_ref,
     own_ref,
@@ -51,6 +52,7 @@
     soft_ref,
     context_ref,
     inputs_v,
+    shaped_v,
     normed_v,
     w_v,
     span_v,
@@ -99,7 +101,7 @@
             mode = jnp.where(kind == 0, table[0:1], jnp.where(kind == 1, table[1:2], table[2:3]))
             shaped = jnp.where(span[r], sentinel, inputs_v[r, :, at].astype(F32) + mode)
             shaped = shaped.astype(BF16)
-            shaped_ref[r * length : (r + 1) * length, at] = shaped
+            shaped_v[r * length : (r + 1) * length, at] = shaped
             wide = shaped.astype(F32)
             wide = wide * wide
             for k in range(0, chunk, 128):
@@ -109,7 +111,7 @@
     inv_rms = lax.rsqrt(mean + 1e-06)
     for c in range(chunks):
         at = pl.ds(c * chunk, chunk)
-        normed_v[:, at] = (shaped_ref[:, at].astype(F32) * inv_rms).astype(BF16)
+        normed_v[:, at] = (shaped_v[:, at].astype(F32) * inv_rms).astype(BF16)
 
     t_at = lax.broadcasted_iota(jnp.int32, (length, 128), 0)
     lane = lax.broadcasted_iota(jnp.int32, (length, 128), 1)
@@ -127,6 +129,8 @@
         marks = jnp.where((lane == 4) & valid & (move == 0), 1.0, marks)
         marks_ref[here, :] = jnp.where(lane == 5, jnp.maximum(count, 1).astype(F32), marks)
 
+    order = order_rows(tokens, rows, members)
+    ordered_ref[...] = dot(order, shaped_v[...], ((1,), (0,))).astype(BF16)
     marks = marks_ref[...]
     head = w_v.shape[2]
 
@@ -171,42 +175,49 @@
     piece = rows * per_row
     row_at = lax.broadcasted_iota(jnp.int32, (tokens, tokens), 0)
     from_at = lax.broadcasted_iota(jnp.int32, (tokens, tokens), 1)
-    mine = lax.rem(lax.axis_index("mp"), WINDOW)
+    member_at = lax.axis_index("mp")
+    mine = lax.rem(member_at, WINDOW)
+    step = jnp.where(lax.rem(member_at, 2) == 0, 1, WINDOW - 1)
     want = jnp.full((tokens, tokens), -1, jnp.int32)
     for i in range(tokens // per_row):
         block, left = divmod(i, tokens // WINDOW // per_row)
         j, r = divmod(left, rows)
-        member = WINDOW * j + lax.rem(mine + block, WINDOW)
+        member = WINDOW * j + lax.rem(mine + block * step, WINDOW)
         first = r * (tokens // rows) + member * per_row
         here = (row_at >= i * per_row) & (row_at < (i + 1) * per_row)
         want = jnp.where(here, first + row_at - i * per_row, want)
     return jnp.where(from_at == want, 1.0, 0.0).astype(BF16)
 
 
-def emit(chunk, rows, gradients, turned_ref, shaped_ref, inv_rms, inner, keep, out_refs):
-    tokens, width = shaped_ref.shape
+def emit(rows, gradients, turned_ref, ordered_ref, inv_rms, inner, keep, out_refs):
+    tokens = ordered_ref.shape[0]
     pieces, piece, _ = out_refs[0].shape
+    order = order_rows(tokens, rows, pieces * WINDOW)
+    lane = lax.broadcasted_iota(jnp.int32, (tokens, 128), 1)
     scale = jnp.where(keep, inv_rms, 0.0)
-    back = inv_rms * inner
-    order = order_rows(tokens, rows, pieces * WINDOW)
-    for c in range(width // chunk):
-        at = pl.ds(c * chunk, chunk)
-        total = None
-        for i in range(3):
-            part = dot(gradients[i], turned_ref[i, :, at], ((1,), (0,)))
-            total = part if total is None else total + part
-        part = ((total - shaped_ref[:, at].astype(F32) * back) * scale).astype(BF16)
-        part = dot(order, part, ((1,), (0,)))
-        for s in range(WINDOW):
-            for j in range(pieces):
-                low = (s * pieces + j) * piece
-                out_refs[s][j, :, at] = part[low : low + piece].astype(BF16)
+    columns = jnp.where(lane == 0, scale, jnp.where(lane == 1, inv_rms * inner, 0.0))
+    columns = lax.dot_general(
+        order.astype(F32),
+        columns,
+        (((1,), (0,)), ((), ())),
+        precision=lax.Precision.HIGHEST,
+        preferred_element_type=F32,
+    )
+    total = None
+    for i in range(3):
+        gradient = dot(order, gradients[i], ((1,), (0,))).astype(BF16)
+        part = dot(gradient, turned_ref[i], ((1,), (0,)))
+        total = part if total is None else total + part
+    part = (total - ordered_ref[...].astype(F32) * columns[:, 1:2]) * columns[:, 0:1]
+    for s in range(WINDOW):
+        for j in range(pieces):
+            low = (s * pieces + j) * piece
+            out_refs[s][j] = part[low : low + piece].astype(BF16)
 
 
 def backward(
-    chunk,
     turned_ref,
-    shaped_ref,
+    ordered_ref,
     marks_ref,
     wide_ref,
     soft_ref,
@@ -215,7 +226,7 @@
     got_mate_ref,
     *out_refs,
 ):
-    tokens, width = shaped_ref.shape
+    tokens, width = ordered_ref.shape
     rows = tokens // got_mate_ref.shape[1]
     head = turned_ref.shape[1]
 
@@ -246,15 +257,15 @@
     gradients = (grad_query, grad_key, grad_value)
     inner = sum(gradients[i].astype(F32) * wide_ref[i] for i in range(3))
     inner = jnp.sum(inner, axis=1, keepdims=True) * (1.0 / width)
-    emit(chunk, rows, gradients, turned_ref, shaped_ref, inv_rms, inner, marks[:, 3:4] == 1.0, out_refs)
+    emit(rows, gradients, turned_ref, ordered_ref, inv_rms, inner, marks[:, 3:4] == 1.0, out_refs)
 
 
 def combine(
-    keep_ref, got_left_ref, got_right_ref, context_ref, got_mate_ref, out_ref, pay_other_ref
+    keep_ref, got_first_ref, got_second_ref, context_ref, got_mate_ref, out_ref, pay_other_ref
 ):
     del got_mate_ref
-    total = keep_ref[...].astype(F32) + got_left_ref[...].astype(F32)
-    out_ref[...] = (total + got_right_ref[...].astype(F32)).astype(BF16)
+    total = keep_ref[...].astype(F32) + got_first_ref[...].astype(F32)
+    out_ref[...] = (total + got_second_ref[...].astype(F32)).astype(BF16)
     rows = context_ref.shape[0] // 2
     pay_other_ref[...] = jnp.where(is_even(), context_ref[rows + 1], context_ref[rows])
 
@@ -280,6 +291,10 @@
     per_row = out_ref.shape[1]
     for r in range(out_ref.shape[0]):
         out_ref[r] = total[r * per_row : (r + 1) * per_row].astype(BF16)
+
+
+def ring_pairs(size):
+    return [(i, (i + 1) % size if i % 2 else (i - 1) % size) for i in range(size)]
 
 
 def exchange(array, pairs):
@@ -310,7 +325,7 @@
     hbm = pl.BlockSpec(memory_space=pltpu.HBM)
     params = pltpu.CompilerParams(vmem_limit_bytes=24 * MIB)
     mates = [(g, g ^ 1) for g in range(groups)]
-    others = [(g, (g + 1) % groups if g % 2 else (g - 1) % groups) for g in range(groups)]
+    others = ring_pairs(groups)
 
     def shape(dims, dtype):
         return jax.ShapeDtypeStruct(dims, dtype)
@@ -319,7 +334,7 @@
     cotangent_mate = exchange(cotangent, mates)
     cotangent_other = exchange(cotangent, others)
     shaped, turned, marks, own, wide, soft, context = pl.pallas_call(
-        lambda *refs: forward(chunk, *refs),
+        lambda *refs: forward(chunk, members, *refs),
         out_shape=(
             shape((tokens, width), BF16),
             shape((3, head, width), BF16),
@@ -333,6 +348,7 @@
         out_specs=[vmem] * 7,
         scratch_shapes=[
             pltpu.VMEM((rows, length, width), BF16),
+            pltpu.VMEM((tokens, width), BF16),
             pltpu.VMEM((tokens, width), BF16),
             pltpu.VMEM((3, width, head), BF16),
             pltpu.VMEM(span_mask.shape, jnp.int32),
@@ -366,16 +382,16 @@
     )
 
     part = shape((members // WINDOW, rows * seg, width), BF16)
-    keep, to_right, to_left = pl.pallas_call(
-        lambda *refs: backward(width, *refs),
+    keep, to_first, to_second = pl.pallas_call(
+        backward,
         out_shape=(part, part, part),
         in_specs=[vmem] * 8,
         out_specs=[vmem] * 3,
         compiler_params=params,
         name="backward",
     )(turned, shaped, marks, wide, soft, own, cotangent_other, cotangent_mate)
-    from_left = lax.ppermute(to_right, "mp", [(m, (m + 1) % members) for m in range(members)])
-    from_right = lax.ppermute(to_left, "mp", [(m, (m - 1) % members) for m in range(members)])
+    from_first = lax.ppermute(to_first, "mp", [(m, m ^ 1) for m in range(members)])
+    from_second = lax.ppermute(to_second, "mp", ring_pairs(members))
     pay_mate = pl.pallas_call(
         address,
         out_shape=slot,
@@ -392,7 +408,7 @@
         out_specs=[vmem] * 2,
         compiler_params=params,
         name="combine",
-    )(keep, from_left, from_right, context, got_mate)
+    )(keep, from_first, from_second, context, got_mate)
     got_other = exchange(pay_other, others)
     spread = [list(range(c, members, WINDOW)) for c in range(WINDOW)]
     heads = lax.all_to_all(windows, "mp", 0, 0, axis_index_groups=spread)

time: 59.6 us -> 60 us (level)
  the two profiles are of different devices: /device:TPU:60 before, /device:TPU:56 now
where the time goes in v7:
time: 60 us; the launch traced here: 59.7 us
  starting transfers between devices  31.6 us (53%)
  waiting for transfers between devices  19.6 us (33%)
  Pallas kernels  7.82 us (13%)
  between operations  0.72 us (1%)
    ppermute x1, starting transfers between devices, shards(): from_second = lax.ppermute(to_second, 'mp', ring_pairs(members))  12.8 us
    all_to_all x1, waiting for transfers between devices, shards(): heads = lax.all_to_all(windows, 'mp', 0, 0, axis_index_groups=spread)  11.6 us
    ppermute x4, starting transfers between devices, exchange(): return lax.ppermute(array, 'dp', pairs)  9.43 us
    all_to_all x1, starting transfers between devices, shards(): heads = lax.all_to_all(windows, 'mp', 0, 0, axis_index_groups=spread)  5.08 us
    pallas_call x1, Pallas kernels, shards(): pl.pallas_call(lambda *refs: forward(chunk, members, *refs), out_shape=(s...  4.46 us
    ppermute x1, starting transfers between devices, shards(): lax.ppermute(to_first, 'mp', [(m, m ^ 1) for m in range(members)])  4.28 us
    ppermute x4, waiting for transfers between devices, exchange(): return lax.ppermute(array, 'dp', pairs)  4.06 us
    ppermute x1, waiting for transfers between devices, shards(): from_second = lax.ppermute(to_second, 'mp', ring_pairs(members))  3.95 us
  transfers between devices with their start and end apart: 7, of which 4 were waited for; matrix products, arithmetic and copies ran while one was open for 0% of the time, Pallas kernels for 8%

profile of v7, /device:TPU:56, one launch (start us, length us, event | category | flops | bytes accessed | tf_op | source)
XLA Modules:
  0.0 59.7 jit_solution(15670367426184206042)
XLA Ops:
  0.6 1.9 %collective-permute-start.1 = (bf16[4,48,256]{2,1,0:T(8,128)(2,1)}, bf16[4,48,256]{2,1,0:T(8,128)(2,1)S(1)}, u32[]{:S(2)}, u32[]{:S(2)}) collective-permute-start(bf16[4,48,256]{2,1,0:T(8,128)(2,1)} %refs_7_.1), channel_id=1, source_target_pairs={{0,12},{12,0},{24,36},{36,24},{48,60},{60,48},{72,84},{84,72},{96,... | collective-permute-start | bytes 294920 | tf_op jit(solution)/shard_map/ppermute | solution.py:301
  2.6 3.4 %collective-permute-start = (bf16[4,48,256]{2,1,0:T(8,128)(2,1)}, bf16[4,48,256]{2,1,0:T(8,128)(2,1)S(1)}, u32[]{:S(2)}, u32[]{:S(2)}) collective-permute-start(bf16[4,48,256]{2,1,0:T(8,128)(2,1)} %refs_7_.1), channel_id=1, source_target_pairs={{0,756},{12,24},{24,12},{36,48},{48,36},{60,72},{72,60},{84,96},{9... | collective-permute-start | bytes 294920 | tf_op jit(solution)/shard_map/ppermute | solution.py:301
  5.9 4.5 %forward.1 = (bf16[96,4096]{1,0:T(8,128)(2,1)S(1)}, bf16[3,256,4096]{2,1,0:T(8,128)(2,1)S(1)}, f32[96,128]{1,0:T(8,128)S(1)}, bf16[96,256]{1,0:T(8,128)(2,1)S(1)...) custom-call(bf16[2,48,4096]{2,1,0:T(8,128)(2,1)} %refs_0_.1, s32[2]{0:T(128)} %refs_1_.1, ...), custom_call_target="tpu_custom_call" | custom-call | tf_op jit(solution)/shard_map/forward/pallas_call | solution.py:336
  10.4 0.0 collective-permute-done.1.got_mate_ref
  10.4 0.0 collective-permute-done.got_other_ref
  10.4 1.8 %backward.1 = (bf16[4,8,4096]{2,1,0:T(8,128)(2,1)S(1)}, bf16[4,8,4096]{2,1,0:T(8,128)(2,1)S(1)}, bf16[4,8,4096]{2,1,0:T(8,128)(2,1)S(1)}) custom-call(bf16[3,256,4096]{2,1,0:T(8,128)(2,1)S(1)} %get-tuple-element.14.turned_ref, bf16[96,4096]{1,0:T(8,128)(2,1)S(1)} %get-tuple-element.15.ordered_ref, f32[96,128]{1,0:T(8,128)S(1)} %get-tuple-element.16.marks_ref, ...), custom_call_target="tpu_custom_call" | custom-call | tf_op jit(solution)/shard_map/backward/pallas_call | solution.py:385
  12.3 4.3 %collective-permute-start.2 = (bf16[4,8,4096]{2,1,0:T(8,128)(2,1)S(1)}, bf16[4,8,4096]{2,1,0:T(8,128)(2,1)S(1)}, u32[]{:S(2)}, u32[]{:S(2)}) collective-permute-start(bf16[4,8,4096]{2,1,0:T(8,128)(2,1)S(1)} %get-tuple-element.21), channel_id=1, source_target_pairs={{0,1},{1,0},{2,3},{3,2},{4,5},{5,4},{6,7},{7,6},{8,9},{9,8},{10,11... | collective-permute-start | bytes 786440 | tf_op jit(solution)/shard_map/ppermute | solution.py:393
  16.6 12.8 %collective-permute-start.3 = (bf16[4,8,4096]{2,1,0:T(8,128)(2,1)S(1)}, bf16[4,8,4096]{2,1,0:T(8,128)(2,1)S(1)}, u32[]{:S(2)}, u32[]{:S(2)}) collective-permute-start(bf16[4,8,4096]{2,1,0:T(8,128)(2,1)S(1)} %get-tuple-element.22), channel_id=1, source_target_pairs={{0,11},{1,2},{2,1},{3,4},{4,3},{5,6},{6,5},{7,8},{8,7},{9,10},{10,... | collective-permute-start | bytes 786440 | tf_op jit(solution)/shard_map/ppermute | solution.py:394
  29.4 2.2 %collective-permute-start.4 = (bf16[48,256]{1,0:T(8,128)(2,1)S(1)}, bf16[48,256]{1,0:T(8,128)(2,1)S(1)}, u32[]{:S(2)}, u32[]{:S(2)}) collective-permute-start(bf16[48,256]{1,0:T(8,128)(2,1)S(1)} %address.1), channel_id=1, source_target_pairs={{0,12},{12,0},{24,36},{36,24},{48,60},{60,48},{72,84},{84,72},{96,... | collective-permute-start | bytes 73736 | tf_op jit(solution)/shard_map/ppermute | solution.py:301
  31.6 0.8 %collective-permute-done.4.got_mate_ref = bf16[48,256]{1,0:T(8,128)(2,1)S(1)} collective-permute-done((bf16[48,256]{1,0:T(8,128)(2,1)S(1)}, bf16[48,256]{1,0:T(8,128)(2,1)S(1)}, u32[]{:S(2)}, u32[]{:S(2)}) %collective-permute-start.4) | collective-permute-done | bytes 24608 | tf_op jit(solution)/shard_map/ppermute | solution.py:301
  32.4 0.0 collective-permute-done.2.got_first_ref
  32.5 4.0 %collective-permute-done.3.got_second_ref = bf16[4,8,4096]{2,1,0:T(8,128)(2,1)S(1)} collective-permute-done((bf16[4,8,4096]{2,1,0:T(8,128)(2,1)S(1)}, bf16[4,8,4096]{2,1,0:T(8,128)(2,1)S(1)}, u32[]{:S(2)}, u32[]{:S(2)}) %collective-permute-start.3) | collective-permute-done | bytes 262176 | tf_op jit(solution)/shard_map/ppermute | solution.py:394
  36.4 0.8 %combine.1 = (bf16[4,8,4096]{2,1,0:T(8,128)(2,1)}, bf16[48,256]{1,0:T(8,128)(2,1)S(1)}) custom-call(bf16[4,8,4096]{2,1,0:T(8,128)(2,1)S(1)} %get-tuple-element.20.keep_ref, bf16[4,8,4096]{2,1,0:T(8,128)(2,1)S(1)} %collective-permute-done.2.got_first_ref, bf16[4,8,4096]{2,1,0:T(8,128)(2,1)S(1)} %collective-permute-done.3.got_second_ref, ...), custom_call_target="tpu_custom_call" | custom-call | tf_op jit(solution)/shard_map/combine/pallas_call | solution.py:404
  37.2 5.1 %all-to-all-start = ((bf16[4,8,4096]{2,1,0:T(8,128)(2,1)}), bf16[4,8,4096]{2,1,0:T(8,128)(2,1)S(1)}, u32[]{:S(2)}, u32[]{:S(2)}) async-start(bf16[4,8,4096]{2,1,0:T(8,128)(2,1)} %get-tuple-element.24), calls=%async_computation | async-start | bytes 524288 | tf_op jit(solution)/shard_map/all_to_all | solution.py:414
  42.3 1.9 %collective-permute-start.5 = (bf16[48,256]{1,0:T(8,128)(2,1)S(1)}, bf16[48,256]{1,0:T(8,128)(2,1)S(1)}, u32[]{:S(2)}, u32[]{:S(2)}) collective-permute-start(bf16[48,256]{1,0:T(8,128)(2,1)S(1)} %get-tuple-element.25), channel_id=1, source_target_pairs={{0,756},{12,24},{24,12},{36,48},{48,36},{60,72},{72,60},{84,96},{9... | collective-permute-start | bytes 73736 | tf_op jit(solution)/shard_map/ppermute | solution.py:301
  44.2 3.2 %collective-permute-done.5.got_other_ref = bf16[48,256]{1,0:T(8,128)(2,1)S(1)} collective-permute-done((bf16[48,256]{1,0:T(8,128)(2,1)S(1)}, bf16[48,256]{1,0:T(8,128)(2,1)S(1)}, u32[]{:S(2)}, u32[]{:S(2)}) %collective-permute-start.5) | collective-permute-done | bytes 24608 | tf_op jit(solution)/shard_map/ppermute | solution.py:301
  47.4 11.6 %all-to-all-done.heads_ref = bf16[4,8,4096]{2,1,0:T(8,128)(2,1)S(1)} async-done(((bf16[4,8,4096]{2,1,0:T(8,128)(2,1)}), bf16[4,8,4096]{2,1,0:T(8,128)(2,1)S(1)}, u32[]{:S(2)}, u32[]{:S(2)}) %all-to-all-start) | async-done | bytes 262176 | tf_op jit(solution)/shard_map/all_to_all | solution.py:414
  59.0 0.7 %finish.1 = (bf16[4,48,256]{2,1,0:T(8,128)(2,1)}, bf16[2,4,4096]{2,1,0:T(4,128)(2,1)}) custom-call(bf16[4,8,4096]{2,1,0:T(8,128)(2,1)S(1)} %all-to-all-done.heads_ref, bf16[4,48,256]{2,1,0:T(8,128)(2,1)S(1)} %get-tuple-element.23.context_ref, bf16[48,256]{1,0:T(8,128)(2,1)S(1)} %collective-permute-done.4.got_mate_ref, ...), custom_call_target="tpu_custom_call" | custom-call | tf_op jit(solution)/shard_map/finish/pallas_call | solution.py:415
  (1 shorter events, 0.0 us)
Async XLA Ops:
  0.6 9.8 %collective-permute-start.1 = (bf16[4,48,256]{2,1,0:T(8,128)(2,1)}, bf16[4,48,256]{2,1,0:T(8,128)(2,1)S(1)}, u32[]{:S(2)}, u32[]{:S(2)}) collective-permute-start(bf16[4,48,256]{2,1,0:T(8,128)(2,1)} %refs_7_.1), channel_id=1, source_target_pairs={{0,12},{12,0},{24,36},{36,24},{48,60},{60,48},{72,84},{84,72},{96,... | collective-permute-start | bytes 294920 | tf_op jit(solution)/shard_map/ppermute | solution.py:301
  2.6 7.9 %collective-permute-start = (bf16[4,48,256]{2,1,0:T(8,128)(2,1)}, bf16[4,48,256]{2,1,0:T(8,128)(2,1)S(1)}, u32[]{:S(2)}, u32[]{:S(2)}) collective-permute-start(bf16[4,48,256]{2,1,0:T(8,128)(2,1)} %refs_7_.1), channel_id=1, source_target_pairs={{0,756},{12,24},{24,12},{36,48},{48,36},{60,72},{72,60},{84,96},{9... | collective-permute-start | bytes 294920 | tf_op jit(solution)/shard_map/ppermute | solution.py:301
  12.3 20.2 %collective-permute-start.2 = (bf16[4,8,4096]{2,1,0:T(8,128)(2,1)S(1)}, bf16[4,8,4096]{2,1,0:T(8,128)(2,1)S(1)}, u32[]{:S(2)}, u32[]{:S(2)}) collective-permute-start(bf16[4,8,4096]{2,1,0:T(8,128)(2,1)S(1)} %get-tuple-element.21), channel_id=1, source_target_pairs={{0,1},{1,0},{2,3},{3,2},{4,5},{5,4},{6,7},{7,6},{8,9},{9,8},{10,11... | collective-permute-start | bytes 786440 | tf_op jit(solution)/shard_map/ppermute | solution.py:393
  16.6 19.8 %collective-permute-start.3 = (bf16[4,8,4096]{2,1,0:T(8,128)(2,1)S(1)}, bf16[4,8,4096]{2,1,0:T(8,128)(2,1)S(1)}, u32[]{:S(2)}, u32[]{:S(2)}) collective-permute-start(bf16[4,8,4096]{2,1,0:T(8,128)(2,1)S(1)} %get-tuple-element.22), channel_id=1, source_target_pairs={{0,11},{1,2},{2,1},{3,4},{4,3},{5,6},{6,5},{7,8},{8,7},{9,10},{10,... | collective-permute-start | bytes 786440 | tf_op jit(solution)/shard_map/ppermute | solution.py:394
  29.4 3.1 %collective-permute-start.4 = (bf16[48,256]{1,0:T(8,128)(2,1)S(1)}, bf16[48,256]{1,0:T(8,128)(2,1)S(1)}, u32[]{:S(2)}, u32[]{:S(2)}) collective-permute-start(bf16[48,256]{1,0:T(8,128)(2,1)S(1)} %address.1), channel_id=1, source_target_pairs={{0,12},{12,0},{24,36},{36,24},{48,60},{60,48},{72,84},{84,72},{96,... | collective-permute-start | bytes 73736 | tf_op jit(solution)/shard_map/ppermute | solution.py:301
  37.2 21.8 %all-to-all-start = ((bf16[4,8,4096]{2,1,0:T(8,128)(2,1)}), bf16[4,8,4096]{2,1,0:T(8,128)(2,1)S(1)}, u32[]{:S(2)}, u32[]{:S(2)}) async-start(bf16[4,8,4096]{2,1,0:T(8,128)(2,1)} %get-tuple-element.24), calls=%async_computation | async-start | bytes 524288 | tf_op jit(solution)/shard_map/all_to_all | solution.py:414
  42.3 5.1 %collective-permute-start.5 = (bf16[48,256]{1,0:T(8,128)(2,1)S(1)}, bf16[48,256]{1,0:T(8,128)(2,1)S(1)}, u32[]{:S(2)}, u32[]{:S(2)}) collective-permute-start(bf16[48,256]{1,0:T(8,128)(2,1)S(1)} %get-tuple-element.25), channel_id=1, source_target_pairs={{0,756},{12,24},{24,12},{36,48},{48,36},{60,72},{72,60},{84,96},{9... | collective-permute-start | bytes 73736 | tf_op jit(solution)/shard_map/ppermute | solution.py:301
